TPU v7x, 32 devices: a whole 2x2x4 slice. The times are simulated.
32 devices in a mesh: dp: 4 (over z), ctx: 4 (over y, core), tensor: 2 (over x).
Axes of the slice: x: 2, y: 2, z: 4, core: 2. Of those that a mesh axis runs over, the one named last changes fastest.
Arguments:
- tokens: bfloat16 [4096, 4, 2048], P('ctx', 'dp'), may hold values from -6 to 6
- q_weight: bfloat16 [2048, 2048], P(None, 'tensor'), may hold values from -0.125 to 0.125
- k_weight: bfloat16 [2048, 2048], P(None, 'tensor'), may hold values from -0.125 to 0.125
- v_weight: bfloat16 [2048, 2048], P(None, 'tensor'), may hold values from -0.125 to 0.125
- o_weight: bfloat16 [2048, 2048], P(None, 'tensor'), may hold values from -0.125 to 0.125
- gate_weight: bfloat16 [2048, 8192], P(None, 'tensor'), may hold values from -0.125 to 0.125
- up_weight: bfloat16 [2048, 8192], P(None, 'tensor'), may hold values from -0.125 to 0.125
- down_weight: bfloat16 [2048, 8192], P(None, 'tensor'), may hold values from -0.0625 to 0.0625
- q_gain: float32 [2048], P('tensor'), may hold values from 0.3 to 4.5
- k_gain: float32 [2048], P('tensor'), may hold values from 0.3 to 4.5
- attn_gain: float32 [2048], replicated, may hold values from 0.5 to 1.5
- mlp_gain: float32 [2048], replicated, may hold values from 0.5 to 1.5
- group_order: int32 [4, 8], P('dp'), may hold values from 0 to 7, each once within a row
- cotangent: bfloat16 [4096, 4, 2048], P('ctx', 'dp'), may hold values from -6 to 6
Outputs:
- output: bfloat16 [4096, 4, 2048], P('ctx', 'dp')
- input_grad: bfloat16 [4096, 4, 2048], P('ctx', 'dp')
- q_weight_grad: float32 [2048, 2048], P(('dp', 'ctx'), 'tensor')
- k_weight_grad: float32 [2048, 2048], P(('dp', 'ctx'), 'tensor')
- v_weight_grad: float32 [2048, 2048], P(('dp', 'ctx'), 'tensor')
- o_weight_grad: float32 [2048, 2048], P(('dp', 'ctx'), 'tensor')
- gate_weight_grad: float32 [2048, 8192], P(('dp', 'ctx'), 'tensor')
- up_weight_grad: float32 [2048, 8192], P(('dp', 'ctx'), 'tensor')
- down_weight_grad: float32 [2048, 8192], P(('dp', 'ctx'), 'tensor')
- q_gain_grad: float32 [2048], P('tensor')
- k_gain_grad: float32 [2048], P('tensor')
- attn_gain_grad: float32 [2048], replicated
- mlp_gain_grad: float32 [2048], replicated
Inputs may be any that keep to these rules, and one draw needn't show every extreme that they name: `group_order`: each row is a permutation of the 8 block numbers.
All inputs are finite; a program needn't handle non-finite values.
Results may differ from a plain program's by a relative error of at most 0.025.
Values may be sent and summed in bfloat16 or wider, within the bound.
No kernel may reach another device: no remote copies, remote signals or barrier semaphores. Data moves between devices by JAX's collectives and lax.ppermute only.
A program may use at most 576 MiB of HBM per device.

v0:
```python
import jax
import jax.numpy as jnp
from jax import lax
from jax.sharding import PartitionSpec as P

H = 16
HD = 128


EPS = 1e-06
THETA = 500000.0


def plain(left, right):
    return jnp.dot(left, right, preferred_element_type=jnp.float32)


def times_trans(left, right):
    return lax.dot_general(
        left, right, (((1,), (1,)), ((), ())), preferred_element_type=jnp.float32
    )


def row_dot(left, right):
    return lax.dot_general(
        left, right, (((0,), (0,)), ((), ())), preferred_element_type=jnp.float32
    )


def rounded(value):
    return lax.optimization_barrier(value.astype(jnp.bfloat16)).astype(jnp.float32)


def rotate(value, cosine, sine):
    half = value.shape[-1] // 2
    first = value[..., :half]
    second = value[..., half:]
    return jnp.concatenate(
        [first * cosine - second * sine, second * cosine + first * sine], axis=-1
    )


def unrotate(grad, cosine, sine):
    half = grad.shape[-1] // 2
    first = grad[..., :half]
    second = grad[..., half:]
    return jnp.concatenate(
        [first * cosine + second * sine, second * cosine - first * sine], axis=-1
    )


def position_table(group_order, length):
    groups = group_order.shape[1]
    block = length // groups
    slots = jnp.arange(length, dtype=jnp.int32)
    onehot = (slots // block)[:, None] == jnp.arange(groups, dtype=jnp.int32)[None, :]
    picked = jnp.sum(jnp.where(onehot[:, None, :], group_order[None, :, :], 0), axis=-1)
    return picked * block + (slots % block)[:, None]


def branch_total(term, total_rows):
    return lax.psum(term(0, total_rows).astype(jnp.bfloat16), "tensor").astype(jnp.float32)


def branch_gains(attn_term, mlp_term):
    return (attn_term, mlp_term)


def on_device(
    tokens,
    q_weight,
    k_weight,
    v_weight,
    o_weight,
    gate_weight,
    up_weight,
    down_weight,
    q_gain,
    k_gain,
    attn_gain,
    mlp_gain,
    group_order,
    cotangent,
):
    local, seqs, width = tokens.shape
    rows = local * seqs
    heads_here = q_weight.shape[1] // HD
    features = H * HD
    scale = HD ** (-0.5)
    flat = tokens.reshape(rows, width)
    query_raw = plain(flat, q_weight)
    key_raw = plain(flat, k_weight)
    value_raw = plain(flat, v_weight)
    square_sums = lax.psum(
        (jnp.sum(query_raw * query_raw, -1), jnp.sum(key_raw * key_raw, -1)), "tensor"
    )
    q_scale = lax.rsqrt(square_sums[0] / features + EPS)[:, None]
    k_scale = lax.rsqrt(square_sums[1] / features + EPS)[:, None]
    q_normed = query_raw * q_scale * q_gain
    k_normed = key_raw * k_scale * k_gain
    length = local * lax.axis_size("ctx")
    offset = lax.axis_index("ctx") * local
    positions = position_table(group_order, length)
    query_pos = lax.dynamic_slice_in_dim(positions, offset, local, 0)
    freq = jnp.power(THETA, -jnp.arange(HD // 2, dtype=jnp.float32) * 2.0 / HD)
    angle = query_pos.astype(jnp.float32)[..., None] * freq
    cosine = jnp.cos(angle)[:, :, None, :]
    sine = jnp.sin(angle)[:, :, None, :]
    queries = rotate(q_normed.reshape(local, seqs, heads_here, HD), cosine, sine).astype(
        jnp.bfloat16
    )
    keys = rotate(k_normed.reshape(local, seqs, heads_here, HD), cosine, sine).astype(jnp.bfloat16)
    values = value_raw.reshape(local, seqs, heads_here, HD).astype(jnp.bfloat16)
    query_side = jnp.transpose(query_pos)

    def allowed_mask():
        key_pos = jnp.transpose(positions)
        return key_pos[:, None, None, :] <= query_side[:, None, :, None]

    top = jnp.full((seqs, heads_here, local), -1e30, jnp.float32)
    keys_in = lax.all_gather(keys, "ctx", axis=0, tiled=True)
    values_in = lax.all_gather(values, "ctx", axis=0, tiled=True)
    allowed = allowed_mask()
    scores = (
        jnp.einsum("qshd,kshd->shqk", queries, keys_in, preferred_element_type=jnp.float32) * scale
    )
    scores = jnp.where(allowed, scores, -1e30)
    new_top = jnp.maximum(top, jnp.max(scores, axis=-1))
    expo = jnp.where(allowed, jnp.exp(scores - new_top[..., None]), 0.0)
    total = jnp.sum(expo, axis=-1)
    product = jnp.einsum(
        "shqk,kshd->qshd", expo.astype(jnp.bfloat16), values_in, preferred_element_type=jnp.float32
    )
    accum = product
    top, total, accum = (new_top, total, accum)
    log_total = top + jnp.log(total)
    attended = accum / jnp.transpose(total, (2, 0, 1))[..., None]
    attended_low = attended.reshape(rows, heads_here * HD).astype(jnp.bfloat16)

    def attention_term(start, count):
        return times_trans(attended_low, o_weight)

    branch = branch_total(attention_term, rows)
    a_scale = lax.rsqrt(jnp.mean(branch * branch, axis=-1, keepdims=True) + EPS)
    hidden = flat.astype(jnp.float32) + branch * a_scale * attn_gain
    lowered = hidden.astype(jnp.bfloat16)
    gate = plain(lowered, gate_weight)
    up = plain(lowered, up_weight)
    sigmoid = jax.nn.sigmoid(gate)
    silu_gate = gate * sigmoid
    inner = (silu_gate * up).astype(jnp.bfloat16)

    def mixer_term(start, count):
        return times_trans(inner, down_weight)

    mixed = branch_total(mixer_term, rows)
    m_scale = lax.rsqrt(jnp.mean(mixed * mixed, axis=-1, keepdims=True) + EPS)
    output = hidden + mixed * m_scale * mlp_gain
    output_low = output.astype(jnp.bfloat16)
    grad = cotangent.reshape(rows, width).astype(jnp.float32)
    mlp_gain_term = jnp.sum(grad * mixed * m_scale, axis=0)
    weighted = grad * mlp_gain
    d_mixed_own = (
        m_scale * weighted - mixed * m_scale**3 * jnp.mean(weighted * mixed, axis=-1, keepdims=True)
    ).astype(jnp.bfloat16)
    down_grad = row_dot(d_mixed_own, inner)
    d_inner = plain(d_mixed_own, down_weight)
    d_gate = (d_inner * up * (sigmoid + silu_gate * (1.0 - sigmoid))).astype(jnp.bfloat16)
    d_up = (d_inner * silu_gate).astype(jnp.bfloat16)
    gate_grad = row_dot(lowered, d_gate)
    up_grad = row_dot(lowered, d_up)

    def mixer_back_term(start, count):
        return times_trans(d_gate, gate_weight) + times_trans(d_up, up_weight)

    d_hidden = grad + branch_total(mixer_back_term, rows)
    attn_gain_term = jnp.sum(d_hidden * branch * a_scale, axis=0)
    weighted = d_hidden * attn_gain
    d_branch_own = (
        a_scale * weighted
        - branch * a_scale**3 * jnp.mean(weighted * branch, axis=-1, keepdims=True)
    ).astype(jnp.bfloat16)
    o_grad = row_dot(d_branch_own, attended_low)
    d_attended = (
        plain(d_branch_own, o_weight).astype(jnp.bfloat16).reshape(local, seqs, heads_here, HD)
    )
    delta = jnp.transpose(jnp.sum(d_attended.astype(jnp.float32) * attended, axis=-1), (1, 2, 0))
    keys_in = lax.all_gather(keys, "ctx", axis=0, tiled=True)
    values_in = lax.all_gather(values, "ctx", axis=0, tiled=True)
    allowed = allowed_mask()
    scores = (
        jnp.einsum("qshd,kshd->shqk", queries, keys_in, preferred_element_type=jnp.float32) * scale
    )
    weights = jnp.where(allowed, jnp.exp(scores - log_total[..., None]), 0.0)
    d_vals = jnp.einsum(
        "shqk,qshd->kshd",
        weights.astype(jnp.bfloat16),
        d_attended,
        preferred_element_type=jnp.float32,
    )
    d_weights = jnp.einsum(
        "qshd,kshd->shqk", d_attended, values_in, preferred_element_type=jnp.float32
    )
    d_scores = (weights * (d_weights - delta[..., None])).astype(jnp.bfloat16)
    d_query_sum = (
        jnp.einsum("shqk,kshd->qshd", d_scores, keys_in, preferred_element_type=jnp.float32) * scale
    )
    d_keys_part = (
        jnp.einsum("shqk,qshd->kshd", d_scores, queries, preferred_element_type=jnp.float32) * scale
    )
    update = jnp.stack([d_keys_part, d_vals], axis=2)
    grad_table = update
    d_query_sum, grad_table = (d_query_sum, grad_table)
    own_grads = lax.psum_scatter(
        grad_table.astype(jnp.bfloat16), "ctx", scatter_dimension=0, tiled=True
    ).astype(jnp.float32)
    d_qnorm = unrotate(rounded(d_query_sum), cosine, sine).reshape(rows, heads_here * HD)
    d_knorm = unrotate(rounded(own_grads[:, :, 0]), cosine, sine).reshape(rows, heads_here * HD)
    d_value = own_grads[:, :, 1].astype(jnp.bfloat16).reshape(rows, heads_here * HD)
    q_gain_term = jnp.sum(d_qnorm * query_raw * q_scale, axis=0)
    k_gain_term = jnp.sum(d_knorm * key_raw * k_scale, axis=0)
    q_weighted = d_qnorm * q_gain
    k_weighted = d_knorm * k_gain
    back_sums = lax.psum(
        (jnp.sum(q_weighted * query_raw, -1), jnp.sum(k_weighted * key_raw, -1)), "tensor"
    )
    d_qraw = (
        q_scale * q_weighted - query_raw * q_scale**3 * (back_sums[0] / features)[:, None]
    ).astype(jnp.bfloat16)
    d_kraw = (
        k_scale * k_weighted - key_raw * k_scale**3 * (back_sums[1] / features)[:, None]
    ).astype(jnp.bfloat16)
    q_grad = row_dot(flat, d_qraw)
    k_grad = row_dot(flat, d_kraw)
    v_grad = row_dot(flat, d_value)

    def input_term(start, count):
        total_part = times_trans(d_qraw, q_weight)
        total_part = total_part + times_trans(d_kraw, k_weight)
        return total_part + times_trans(d_value, v_weight)

    d_input = d_hidden + branch_total(input_term, rows)
    input_low = d_input.astype(jnp.bfloat16)
    totals = (
        lax.psum_scatter(
            q_grad.astype(jnp.bfloat16), ("dp", "ctx"), scatter_dimension=0, tiled=True
        ).astype(jnp.float32),
        lax.psum_scatter(
            k_grad.astype(jnp.bfloat16), ("dp", "ctx"), scatter_dimension=0, tiled=True
        ).astype(jnp.float32),
        lax.psum_scatter(
            v_grad.astype(jnp.bfloat16), ("dp", "ctx"), scatter_dimension=0, tiled=True
        ).astype(jnp.float32),
        lax.psum_scatter(
            o_grad.astype(jnp.bfloat16), ("dp", "ctx"), scatter_dimension=0, tiled=True
        ).astype(jnp.float32),
        lax.psum_scatter(
            gate_grad.astype(jnp.bfloat16), ("dp", "ctx"), scatter_dimension=0, tiled=True
        ).astype(jnp.float32),
        lax.psum_scatter(
            up_grad.astype(jnp.bfloat16), ("dp", "ctx"), scatter_dimension=0, tiled=True
        ).astype(jnp.float32),
        lax.psum_scatter(
            down_grad.astype(jnp.bfloat16), ("dp", "ctx"), scatter_dimension=0, tiled=True
        ).astype(jnp.float32),
    )
    attn_gain_part, mlp_gain_part = branch_gains(attn_gain_term, mlp_gain_term)
    gain_totals = lax.psum((q_gain_term, k_gain_term, attn_gain_part, mlp_gain_part), ("dp", "ctx"))
    output_out = output_low.reshape(local, seqs, width)
    input_out = input_low.reshape(local, seqs, width)
    return (
        output_out,
        input_out,
        totals[0],
        totals[1],
        totals[2],
        totals[3],
        totals[4],
        totals[5],
        totals[6],
        gain_totals[0],
        gain_totals[1],
        gain_totals[2],
        gain_totals[3],
    )


def solution(mesh):
    in_specs = (
        P("ctx", "dp", None),
        P(None, "tensor"),
        P(None, "tensor"),
        P(None, "tensor"),
        P(None, "tensor"),
        P(None, "tensor"),
        P(None, "tensor"),
        P(None, "tensor"),
        P("tensor"),
        P("tensor"),
        P(),
        P(),
        P("dp", None),
        P("ctx", "dp", None),
    )
    out_specs = (
        P("ctx", "dp", None),
        P("ctx", "dp", None),
        P(("dp", "ctx"), "tensor"),
        P(("dp", "ctx"), "tensor"),
        P(("dp", "ctx"), "tensor"),
        P(("dp", "ctx"), "tensor"),
        P(("dp", "ctx"), "tensor"),
        P(("dp", "ctx"), "tensor"),
        P(("dp", "ctx"), "tensor"),
        P("tensor"),
        P("tensor"),
        P(),
        P(),
    )
    return jax.shard_map(
        on_device, mesh=mesh, in_specs=in_specs, out_specs=out_specs, check_vma=False
    )
```

profile of v0, /device:TPU:0, one launch (start us, length us, event | category | flops | bytes accessed | tf_op | source)
XLA Modules:
  0.0 2099.6 jit_solution(5845926871077465182)
XLA Ops:
  86.8 39.7 %all-gather.4.cloned.1.call-done = bf16[4096,1,8,128]{3,0,2,1:T(8,128)(2,1)} async-done(((bf16[1024,1,8,128]{3,0,2,1:T(8,128)(2,1)}), bf16[4096,1,8,128]{3,0,2,1:T(8,128)(2,1)}) %all-gather.4.cloned.1.call-update) | async-done | bytes 8388624 | tf_op jit(solution)/shard_map/all_gather | solution.py:121
  126.5 56.7 %select_reduce_fusion = (f32[8,1024]{1,0:T(8,128)S(1)}, f32[8,1024,4096]{2,1,0:T(8,128)}) fusion(pred[1024,4096]{1,0:T(8,128)(4,1)} %broadcast_compare_fusion, bf16[4096,1,8,128]{3,0,2,1:T(8,128)(2,1)} %all-gather.4.cloned.1.call-done, bf16[1024,8,64]{2,0,1:T(8,128)(2,1)} %get-tuple-element.86, bf16[1024,8,64]{2,0,1:T(8,128)(2,1)S(1)} %get-tuple-element.85), kind=kOutput, calls=%fused_computation.3 | convolution fusion | flops 8694784000 | bytes 148930560 | tf_op jit(solution)/shard_map/qshd,kshd->shqk/dot_general | solution.py:125
  183.3 46.6 %fusion.1 = f32[8,1024]{1,0:T(8,128)S(1)} fusion(f32[8,1024,4096]{2,1,0:T(8,128)} %get-tuple-element.122, f32[8,1024]{1,0:T(8,128)S(1)} %broadcast_maximum_fusion, pred[1024,4096]{1,0:T(8,128)(4,1)} %broadcast_compare_fusion), kind=kLoop, calls=%fused_computation.5 | loop fusion | flops 167763968 | bytes 138477568 | tf_op jit(solution)/shard_map/reduce_sum | solution.py:130
  229.9 60.4 %fusion.99 = (bf16[1024,1,8,128]{0,3,2,1:T(8,128)(2,1)S(1)}, f32[1024,1,8,128]{0,3,2,1:T(8,128)}) fusion(f32[1024,8]{0,1:T(8,128)S(1)} %bitcast.189, bf16[4096,8,128]{2,0,1:T(8,128)(2,1)} %all-gather.6.cloned.1.call-done, f32[8,1024,4096]{2,1,0:T(8,128)} %get-tuple-element.122, f32[8,1024]{1,0:T(8,128)S(1)} %broadcast_maximum_fusion, ...), kind=kOutput, calls=%fused_computation.169 | convolution fusion | flops 8759803904 | bytes 153157632 | tf_op jit(solution)/shard_map/shqk,kshd->qshd/dot_general | solution.py:131
  299.4 108.0 %all-reduce.8.cloned.1.call-done = bf16[1024,2048]{1,0:T(8,128)(2,1)} async-done(((bf16[1024,2048]{1,0:T(8,128)(2,1)}), bf16[1024,2048]{1,0:T(8,128)(2,1)}) %all-reduce.8.cloned.1.call-update) | async-done | bytes 4194320 | tf_op jit(solution)/shard_map/psum | solution.py:62
  439.8 29.4 %multiply_convert_fusion.4 = (bf16[1024,4096]{1,0:T(8,128)(2,1)}, f32[1024,4096]{1,0:T(8,128)}) fusion(f32[1024,4096]{1,0:T(8,128)} %fusion.100, bf16[1024,2048]{1,0:T(8,128)(2,1)S(1)} %fusion.36, bf16[2048,4096]{1,0:T(8,128)(2,1)} %param.20), kind=kOutput, calls=%fused_computation.20 | convolution fusion | flops 17205035008 | bytes 62914560 | tf_op jit(solution)/shard_map/dot_general | solution.py:15
  493.5 108.0 %all-reduce.10.cloned.1.call-done = bf16[1024,2048]{1,0:T(8,128)(2,1)} async-done(((bf16[1024,2048]{1,0:T(8,128)(2,1)}), bf16[1024,2048]{1,0:T(8,128)(2,1)}) %all-reduce.10.cloned.1.call-update) | async-done | bytes 4194320 | tf_op jit(solution)/shard_map/psum | solution.py:62
  610.5 33.2 %multiply_convert_fusion.2 = (bf16[1024,4096]{1,0:T(8,128)(2,1)}, bf16[1024,4096]{1,0:T(8,128)(2,1)}) fusion(f32[1024,4096]{1,0:T(8,128)} %fusion.100, f32[1024,4096]{1,0:T(8,128)} %get-tuple-element.126, bf16[2048,4096]{1,0:T(8,128)(2,1)} %param.21, bf16[1024,2048]{1,0:T(8,128)(2,1)} %all-reduce.10.cloned.1.call-done, bf16[1024,1,2048]{2,0,1:T(8,128)(2,1)} %param.27, ...), kind=kOutput, calls=%fused_computation.13 | convolution fusion | flops 17246978048 | bytes 75517952 | tf_op jit(solution)/shard_map/dot_general | solution.py:15
  687.8 107.3 %all-reduce.12.cloned.1.call-done = bf16[1024,2048]{1,0:T(8,128)(2,1)} async-done(((bf16[1024,2048]{1,0:T(8,128)(2,1)}), bf16[1024,2048]{1,0:T(8,128)(2,1)}) %all-reduce.12.cloned.1.call-update) | async-done | bytes 4194320 | tf_op jit(solution)/shard_map/psum | solution.py:62
  821.6 53.8 %convert_bitcast_fusion = bf16[4096,1,1,8,128]{4,0,3,2,1:T(8,128)(2,1)} fusion(bf16[1024,8,128]{0,2,1:T(8,128)(2,1)S(1)} %bitcast.185, f32[8,1024,4096]{2,1,0:T(8,128)} %get-tuple-element.122, f32[8,1024]{1,0:T(8,128)S(1)} %log_add_fusion, pred[1024,4096]{1,0:T(8,128)(4,1)} %broadcast_compare_fusion), kind=kOutput, calls=%fused_computation.59 | convolution fusion | flops 8728346624 | bytes 148930560 | tf_op jit(solution)/shard_map/shqk,qshd->kshd/dot_general | solution.py:195
  875.3 81.8 %multiply_convert_fusion = bf16[8,1024,4096]{2,1,0:T(8,128)(2,1)} fusion(f32[8,1024,4096]{2,1,0:T(8,128)} %get-tuple-element.122, f32[8,1024]{1,0:T(8,128)S(1)} %bitcast.190, f32[8,1024]{1,0:T(8,128)S(1)} %log_add_fusion, pred[1024,4096]{1,0:T(8,128)(4,1)} %broadcast_compare_fusion, bf16[1024,8,128]{0,2,1:T(8,128)(2,1)} %bitcast.186, ...), kind=kOutput, calls=%fused_computation | convolution fusion | flops 8791261184 | bytes 216072192 | tf_op jit(solution)/shard_map/qshd,kshd->shqk/dot_general | solution.py:201
  957.2 32.9 %fusion.37 = bf16[4096,1,1,8,128]{4,0,3,2,1:T(8,128)(2,1)} fusion(bf16[8,1024,4096]{2,1,0:T(8,128)(2,1)} %multiply_convert_fusion, bf16[1024,8,64]{2,0,1:T(8,128)(2,1)} %get-tuple-element.86, bf16[1024,8,64]{2,0,1:T(8,128)(2,1)S(1)} %copy-done.20), kind=kOutput, calls=%fused_computation.63 | convolution fusion | flops 8602517504 | bytes 77594624 | tf_op jit(solution)/shard_map/shqk,qshd->kshd/dot_general | solution.py:209
  1014.6 29.9 %convolution_convert_fusion = bf16[2048,4096]{1,0:T(8,128)(2,1)} fusion(bf16[1024,4096]{1,0:T(8,128)(2,1)} %get-tuple-element.125, bf16[1024,2048]{1,0:T(8,128)(2,1)} %all-reduce.10.cloned.1.call-done, bf16[1024,1,2048]{2,0,1:T(8,128)(2,1)} %param.27, f32[1024]{0:T(1024)S(1)} %copy-done.51, f32[1024]{0:T(1024)S(1)} %copy-done.49, f32[2048]{0:T(1024)S(1)} %copy-done.42, ...), kind=kOutput, calls=%fused_computation.27 | convolution fusion | flops 17205035008 | bytes 33574912 | tf_op jit(solution)/shard_map/dot_general | solution.py:25
  1044.5 25.2 %convolution_convert_fusion.1 = bf16[2048,4096]{1,0:T(8,128)(2,1)} fusion(bf16[1024,2048]{1,0:T(8,128)(2,1)} %copy-done.15, bf16[1024,4096]{1,0:T(8,128)(2,1)} %get-tuple-element.83), kind=kOutput, calls=%fused_computation.28 | convolution fusion | flops 17188257792 | bytes 29360128 | tf_op jit(solution)/shard_map/dot_general | solution.py:25
  1069.8 25.1 %convolution_convert_fusion.2 = bf16[2048,4096]{1,0:T(8,128)(2,1)} fusion(bf16[1024,2048]{1,0:T(8,128)(2,1)} %copy-done.15, bf16[1024,4096]{1,0:T(8,128)(2,1)} %get-tuple-element.84), kind=kOutput, calls=%fused_computation.29 | convolution fusion | flops 17188257792 | bytes 29360128 | tf_op jit(solution)/shard_map/dot_general | solution.py:25
  1095.0 29.0 %fusion.72 = bf16[1024,1,8,128]{3,0,2,1:T(8,128)(2,1)S(1)} fusion(bf16[8,1024,4096]{2,1,0:T(8,128)(2,1)} %multiply_convert_fusion, bf16[4096,1,8,128]{3,0,2,1:T(8,128)(2,1)} %all-gather.4.cloned.1.call-done), kind=kOutput, calls=%fused_computation.121 | convolution fusion | flops 8592031744 | bytes 77594624 | tf_op jit(solution)/shard_map/shqk,kshd->qshd/dot_general | solution.py:206
  1261.1 127.7 %reduce-scatter.23.cloned.1.call-done = bf16[128,4096]{1,0:T(8,128)(2,1)} async-done(((bf16[2048,4096]{1,0:T(8,128)(2,1)}), bf16[128,4096]{1,0:T(8,128)(2,1)}) %reduce-scatter.23.cloned.1.call-update) | async-done | bytes 1048592 | tf_op jit(solution)/shard_map/reduce_scatter | solution.py:263
  1391.6 179.5 %reduce-scatter.21.cloned.1.call-done = bf16[128,4096]{1,0:T(8,128)(2,1)} async-done(((bf16[2048,4096]{1,0:T(8,128)(2,1)}), bf16[128,4096]{1,0:T(8,128)(2,1)}) %reduce-scatter.21.cloned.1.call-update) | async-done | bytes 1048592 | tf_op jit(solution)/shard_map/reduce_scatter | solution.py:260
  1573.9 179.4 %reduce-scatter.19.cloned.1.call-done = bf16[128,4096]{1,0:T(8,128)(2,1)} async-done(((bf16[2048,4096]{1,0:T(8,128)(2,1)}), bf16[128,4096]{1,0:T(8,128)(2,1)}) %reduce-scatter.19.cloned.1.call-update) | async-done | bytes 1048592 | tf_op jit(solution)/shard_map/reduce_scatter | solution.py:257
  1756.1 59.9 %all-reduce = (f32[1024]{0:T(1024)}, f32[1024]{0:T(1024)}, f32[2048]{0:T(1024)}, f32[2048]{0:T(1024)}) all-reduce(f32[1024]{0:T(1024)S(1)} %get-tuple-element.71, f32[1024]{0:T(1024)S(1)} %get-tuple-element.69, f32[2048]{0:T(1024)S(1)} %copy-done.44, f32[2048]{0:T(1024)S(1)} %copy-done.43), channel_id=1, replica_groups=mesh['dp'=4,'ctx'=4,'tensor'=2] {'dp','ctx'}, use_global_device_ids=true, to_apply=%region_29.30 | all-reduce | flops 6144 | bytes 49152 | tf_op jit(solution)/shard_map/psum | solution.py:268
  1816.0 47.4 %all-reduce.14.cloned.1.call-done = bf16[1024,2048]{1,0:T(8,128)(2,1)} async-done(((bf16[1024,2048]{1,0:T(8,128)(2,1)}), bf16[1024,2048]{1,0:T(8,128)(2,1)}) %all-reduce.14.cloned.1.call-update) | async-done | bytes 4194320 | tf_op jit(solution)/shard_map/psum | solution.py:62
  1873.4 66.2 %reduce-scatter.29.cloned.1.call-done = bf16[128,1024]{1,0:T(8,128)(2,1)} async-done(((bf16[2048,1024]{1,0:T(8,128)(2,1)}), bf16[128,1024]{1,0:T(8,128)(2,1)}) %reduce-scatter.29.cloned.1.call-update) | async-done | bytes 262160
  1941.6 73.7 %reduce-scatter.27.cloned.1.call-done = bf16[128,1024]{1,0:T(8,128)(2,1)} async-done(((bf16[2048,1024]{1,0:T(8,128)(2,1)}), bf16[128,1024]{1,0:T(8,128)(2,1)}) %reduce-scatter.27.cloned.1.call-update) | async-done | bytes 262160
  2017.4 73.1 %reduce-scatter.25.cloned.1.call-done = bf16[128,1024]{1,0:T(8,128)(2,1)} async-done(((bf16[2048,1024]{1,0:T(8,128)(2,1)}), bf16[128,1024]{1,0:T(8,128)(2,1)}) %reduce-scatter.25.cloned.1.call-update) | async-done | bytes 262160
  (227 shorter events, 410.7 us)
Async XLA Ops:
  7.2 119.4 %all-gather.4.cloned.1.call-start = ((), (), s32[]{:S(2)}) async-start(), calls=%async_computation.8 | async-start | bytes 10485760 | tf_op jit(solution)/shard_map/all_gather | solution.py:121
  63.8 62.8 %copy-start.19 = (bf16[1024,8,64]{2,0,1:T(8,128)(2,1)}, bf16[1024,8,64]{2,0,1:T(8,128)(2,1)S(1)}, u32[]{:S(2)}) copy-start(bf16[1024,8,64]{2,0,1:T(8,128)(2,1)S(1)} %get-tuple-element.85) | copy-start | bytes 3145732
  66.3 163.6 %all-gather.6.cloned.1.call-start = ((), (), s32[]{:S(2)}) async-start(), calls=%async_computation.18 | async-start | bytes 10485760 | tf_op jit(solution)/shard_map/all_gather | solution.py:122
  82.0 325.5 %all-reduce.8.cloned.1.call-start = ((), (), s32[]{:S(2)}) async-start(), calls=%async_computation.9 | async-start | bytes 8388608 | tf_op jit(solution)/shard_map/psum | solution.py:62
  299.4 112.5 %copy-start.27 = (f32[2048]{0:T(1024)S(1)}, f32[2048]{0:T(1024)}, u32[]{:S(2)}) copy-start(f32[2048]{0:T(1024)} %param.24) | copy-start | bytes 24580
  299.4 302.1 %all-reduce.10.cloned.1.call-start = ((), (), s32[]{:S(2)}) async-start(), calls=%async_computation.10 | async-start | bytes 8388608 | tf_op jit(solution)/shard_map/psum | solution.py:62
  493.4 111.3 %copy-start.41 = (f32[2048]{0:T(1024)S(1)}, f32[2048]{0:T(1024)}, u32[]{:S(2)}) copy-start(f32[2048]{0:T(1024)} %param.25) | copy-start | bytes 24580
  493.4 301.6 %all-reduce.12.cloned.1.call-start = ((), (), s32[]{:S(2)}) async-start(), calls=%async_computation.11 | async-start | bytes 8388608 | tf_op jit(solution)/shard_map/psum | solution.py:62
  604.7 197.7 %copy-start.39 = (f32[1024]{0:T(1024)}, f32[1024]{0:T(1024)S(1)}, u32[]{:S(2)}) copy-start(f32[1024]{0:T(1024)S(1)} %get-tuple-element.116) | copy-start | bytes 12292
  687.0 108.1 %copy-start.28 = (f32[2048]{0:T(1024)S(1)}, f32[2048]{0:T(1024)}, u32[]{:S(2)}) copy-start(f32[2048]{0:T(1024)} %param.24) | copy-start | bytes 24580
  687.0 108.1 %copy-start.34 = (f32[1024]{0:T(1024)S(1)}, f32[1024]{0:T(1024)}, u32[]{:S(2)}) copy-start(f32[1024]{0:T(1024)} %copy-done.33) | copy-start | bytes 12292
  687.0 443.2 %reduce-scatter.15.cloned.1.call-start = ((), (), s32[]{:S(2)}) async-start(), calls=%async_computation.12 | async-start | bytes 20971520 | tf_op jit(solution)/shard_map/reduce_scatter | solution.py:214
  687.8 114.6 %copy-start.47 = (f32[1024]{0:T(1024)S(1)}, f32[1024]{0:T(1024)}, u32[]{:S(2)}) copy-start(f32[1024]{0:T(1024)} %get-tuple-element.113) | copy-start | bytes 12292
  875.3 81.8 %copy-start.20 = (bf16[1024,8,64]{2,0,1:T(8,128)(2,1)S(1)}, bf16[1024,8,64]{2,0,1:T(8,128)(2,1)}, u32[]{:S(2)}) copy-start(bf16[1024,8,64]{2,0,1:T(8,128)(2,1)} %copy-done.19) | copy-start | bytes 3145732
  1003.9 255.4 %reduce-scatter.17.cloned.1.call-start = ((), (), s32[]{:S(2)}) async-start(), calls=%async_computation.14 | async-start | bytes 4456448 | tf_op jit(solution)/shard_map/reduce_scatter | solution.py:254
  1013.9 374.9 %reduce-scatter.23.cloned.1.call-start = ((), (), s32[]{:S(2)}) async-start(), calls=%async_computation.17 | async-start | bytes 17825792 | tf_op jit(solution)/shard_map/reduce_scatter | solution.py:263
  1044.5 526.7 %reduce-scatter.21.cloned.1.call-start = ((), (), s32[]{:S(2)}) async-start(), calls=%async_computation.16 | async-start | bytes 17825792 | tf_op jit(solution)/shard_map/reduce_scatter | solution.py:260
  1069.8 683.5 %reduce-scatter.19.cloned.1.call-start = ((), (), s32[]{:S(2)}) async-start(), calls=%async_computation.15 | async-start | bytes 17825792 | tf_op jit(solution)/shard_map/reduce_scatter | solution.py:257
  1095.0 768.4 %all-reduce.14.cloned.1.call-start = ((), (), s32[]{:S(2)}) async-start(), calls=%async_computation.13 | async-start | bytes 8388608 | tf_op jit(solution)/shard_map/psum | solution.py:62
  1210.7 728.8 %reduce-scatter.29.cloned.1.call-start = ((), (), s32[]{:S(2)}) async-start(), calls=%async_computation.21 | async-start | bytes 4456448
  1227.5 787.8 %reduce-scatter.27.cloned.1.call-start = ((), (), s32[]{:S(2)}) async-start(), calls=%async_computation.20 | async-start | bytes 4456448
  1244.6 846.0 %reduce-scatter.25.cloned.1.call-start = ((), (), s32[]{:S(2)}) async-start(), calls=%async_computation.19 | async-start | bytes 4456448
  1261.1 494.9 %copy-start.43 = (f32[2048]{0:T(1024)S(1)}, f32[2048]{0:T(1024)}, u32[]{:S(2)}) copy-start(f32[2048]{0:T(1024)} %get-tuple-element.67) | copy-start | bytes 24580
  1261.1 494.9 %copy-start.44 = (f32[2048]{0:T(1024)S(1)}, f32[2048]{0:T(1024)}, u32[]{:S(2)}) copy-start(f32[2048]{0:T(1024)} %get-tuple-element.65) | copy-start | bytes 24580
  (48 other events, 464.3 us)
Sparse Core Ops, SparseCore 0:
  66.4 60.0 all-gather.3
  128.7 58.2 all-gather.5
  299.5 107.9 all-reduce.7
  493.5 107.8 all-reduce.9
  687.1 107.8 all-reduce.11
  1004.1 126.1 reduce-scatter.14
  1134.1 72.3 reduce-scatter.16
  1211.1 177.7 reduce-scatter.22
  1393.5 177.5 reduce-scatter.20
  1575.7 177.5 reduce-scatter.18
  1756.5 106.8 all-reduce.13
  1867.1 72.4 reduce-scatter.28
  1943.9 71.3 reduce-scatter.26
  2019.0 71.4 reduce-scatter.24
where the time goes:
time: 2110 us; the launch traced here: 2100 us
  waiting for transfers between devices  1110 us (53%)
  matrix products  653 us (31%)
  other arithmetic  166 us (8%)
  local copies, waits for them, and re-layouts  79.3 us (4%)
  blocking collectives  71 us (3%)
    psum x4, waiting for transfers between devices, branch_total(): lax.psum(term(0, total_rows).astype(jnp.bfloat16), 'tensor')  371 us
    unnamed x17, waiting for transfers between devices  213 us
    reduce_scatter x1, waiting for transfers between devices, on_device(): lax.psum_scatter(up_grad.astype(jnp.bfloat16), ('dp', 'ctx'), scatter_dim...  180 us
    reduce_scatter x1, waiting for transfers between devices, on_device(): lax.psum_scatter(gate_grad.astype(jnp.bfloat16), ('dp', 'ctx'), scatter_d...  179 us
    reduce_scatter x1, waiting for transfers between devices, on_device(): lax.psum_scatter(down_grad.astype(jnp.bfloat16), ('dp', 'ctx'), scatter_d...  128 us
    dot_general x7, matrix products, plain(): return jnp.dot(left, right, preferred_element_type=jnp.float32)  121 us
    dot_general x7, matrix products, row_dot(): lax.dot_general(left, right, (((0,), (0,)), ((), ())), preferred_element_...  117 us
    dot_general x7, matrix products, times_trans(): lax.dot_general(left, right, (((1,), (1,)), ((), ())), preferred_element_...  101 us
  transfers between devices with their start and end apart: 14, of which 12 were waited for; matrix products, arithmetic and copies ran while one was open for 18% of the time, Pallas kernels for 0%

commit v1 on v0

--- a/solution.py
+++ b/solution.py
@@ -1,6 +1,10 @@
+import functools
+
 import jax
 import jax.numpy as jnp
 from jax import lax
+from jax.experimental import pallas as pl
+from jax.experimental.pallas import tpu as pltpu
 from jax.sharding import PartitionSpec as P
 
 H = 16
@@ -9,21 +13,1179 @@
 
 EPS = 1e-06
 THETA = 500000.0
+LOG2E = 1.4426950408889634
+NEG = -1e30
+SHARE = 64
+LONG = 2000
+F32 = jnp.float32
+BF16 = jnp.bfloat16
 
 
 def plain(left, right):
-    return jnp.dot(left, right, preferred_element_type=jnp.float32)
+    return jnp.dot(left, right, preferred_element_type=F32)
 
 
 def times_trans(left, right):
-    return lax.dot_general(
-        left, right, (((1,), (1,)), ((), ())), preferred_element_type=jnp.float32
-    )
+    return lax.dot_general(left, right, (((1,), (1,)), ((), ())), preferred_element_type=F32)
 
 
 def row_dot(left, right):
-    return lax.dot_general(
-        left, right, (((0,), (0,)), ((), ())), preferred_element_type=jnp.float32
+    return lax.dot_general(left, right, (((0,), (0,)), ((), ())), preferred_element_type=F32)
+
+
+def swap(value, axis, step):
+    count = lax.axis_size(axis)
+    return lax.ppermute(value, axis, [(i, i ^ step) for i in range(count)])
+
+
+def tensor_sum(value):
+    if lax.axis_size("tensor") == 2:
+        return value.astype(F32) + swap(value, "tensor", 1).astype(F32)
+    return lax.psum(value, "tensor").astype(F32)
+
+
+def vmem(megabytes):
+    return pltpu.CompilerParams(vmem_limit_bytes=megabytes * 1024 * 1024)
+
+
+def after(value, *gates):
+    return lax.optimization_barrier((value, gates))[0]
+
+
+def tensor_list(value):
+    if lax.axis_size("tensor") == 2:
+        return [value, swap(value, "tensor", 1)]
+    return [lax.psum(value, "tensor")]
+
+
+def tensor_all(value):
+    count = lax.axis_size("tensor")
+    if count == 2:
+        return [value, swap(value, "tensor", 1)]
+    every = lax.all_gather(value, "tensor", axis=0)
+    return [every[i] for i in range(count)]
+
+
+def cost(flops, nbytes, exps=0, weight=1):
+    flops, nbytes = flops * weight, nbytes * weight
+    return pl.CostEstimate(
+        flops=int(flops) // SHARE, bytes_accessed=int(nbytes) // SHARE, transcendentals=int(exps) // SHARE
+    )
+
+
+def rms(value):
+    return lax.rsqrt(jnp.mean(value * value, axis=-1, keepdims=True) + EPS)
+
+
+def half_turn(value):
+    return pltpu.roll(value, HD // 2, 1)
+
+
+def turned_back(grad, cosine, sine):
+    return grad * cosine - half_turn(grad) * sine
+
+
+def col_slice(col_ref, s, h):
+    return pl.ds(pl.multiple_of(col_ref[s] + h * HD, HD), HD)
+
+
+def pieces_kernel(wide, col_ref, x_ref, w_ref, *outs):
+    x = x_ref[...]
+    for s, out in enumerate(outs):
+        cols = pl.ds(pl.multiple_of(col_ref[s], HD), wide)
+        out[...] = plain(x, w_ref[:, cols]).astype(BF16)
+
+
+def project_pieces(col, x, weight, share=1):
+    rows, depth = x.shape
+    width = weight.shape[1]
+    n_ctx = col.shape[0]
+    wide = width // n_ctx
+    tile = min(256, rows)
+    return pl.pallas_call(
+        functools.partial(pieces_kernel, wide),
+        grid_spec=pltpu.PrefetchScalarGridSpec(
+            num_scalar_prefetch=1,
+            grid=(rows // tile,),
+            in_specs=[
+                pl.BlockSpec((tile, depth), lambda i, col: (i, 0)),
+                pl.BlockSpec((depth, width), lambda i, col: (0, 0)),
+            ],
+            out_specs=[pl.BlockSpec((tile, wide), lambda i, col: (i, 0))] * n_ctx,
+        ),
+        out_shape=[jax.ShapeDtypeStruct((rows, wide), BF16)] * n_ctx,
+        compiler_params=vmem(32),
+        cost_estimate=cost(2 * rows * depth * width, 2 * (rows * depth + depth * width), weight=share),
+    )(col, x, weight)
+
+
+def qk_kernel(x_ref, qw_ref, kw_ref, q_ref, k_ref, sums_ref, q_s, k_s):
+    step = pl.program_id(0)
+    x = x_ref[...]
+    lanes = 128
+    for w_ref, out_ref, total in ((qw_ref, q_ref, q_s), (kw_ref, k_ref, k_s)):
+        raw = plain(x, w_ref[...])
+        out_ref[...] = raw
+        square = raw * raw
+        part = square[:, :lanes]
+        for i in range(1, raw.shape[1] // lanes):
+            part += square[:, i * lanes : (i + 1) * lanes]
+
+        @pl.when(step == 0)
+        def _():
+            total[...] = part
+
+        @pl.when(step > 0)
+        def _():
+            total[...] += part
+
+    @pl.when(step == pl.num_programs(0) - 1)
+    def _():
+        sums_ref[0:1, :] = jnp.sum(q_s[...].T, axis=0, keepdims=True)
+        sums_ref[1:2, :] = jnp.sum(k_s[...].T, axis=0, keepdims=True)
+
+
+def qk_project(x, q_weight, k_weight):
+    rows, depth = x.shape
+    width = q_weight.shape[1]
+    tile = min(256, width)
+    column = lambda i: (0, i)
+    return pl.pallas_call(
+        qk_kernel,
+        grid=(width // tile,),
+        in_specs=[pl.BlockSpec((rows, depth), lambda i: (0, 0))]
+        + [pl.BlockSpec((depth, tile), column)] * 2,
+        out_specs=[pl.BlockSpec((rows, tile), column)] * 2
+        + [pl.BlockSpec((2, rows), lambda i: (0, 0))],
+        out_shape=[jax.ShapeDtypeStruct((rows, width), F32)] * 2
+        + [jax.ShapeDtypeStruct((2, rows), F32)],
+        scratch_shapes=[pltpu.VMEM((rows, 128), F32)] * 2,
+        compiler_params=vmem(32),
+        cost_estimate=cost(4 * rows * depth * width, 2 * rows * depth + 4 * depth * width + 8 * rows * width),
+    )(x, q_weight, k_weight)
+
+
+def head_prep_kernel(n_ctx, nh, col_ref, q_ref, k_ref, v_ref, qs_ref, ks_ref, qg_ref, kg_ref, cos_ref, sin_ref, *outs):
+    cosine = cos_ref[...]
+    sine = sin_ref[...]
+    q_scale = qs_ref[...]
+    k_scale = ks_ref[...]
+    for h in range(nh):
+        for s in range(n_ctx):
+            cols = col_slice(col_ref, s, h)
+            out = outs[h * n_ctx + s]
+            q = q_ref[:, cols] * q_scale * qg_ref[:, cols]
+            out[0] = (q * cosine + half_turn(q) * sine).astype(BF16)
+            k = k_ref[:, cols] * k_scale * kg_ref[:, cols]
+            out[1] = (k * cosine + half_turn(k) * sine).astype(BF16)
+            out[2] = v_ref[:, cols]
+
+
+def head_prep(col, q_raw, k_raw, value, q_scale, k_scale, q_gain, k_gain, cosine, sine, n_ctx, nh):
+    rows, width = q_raw.shape
+    tile = min(256, rows)
+    row = lambda i, col: (i, 0)
+    fixed = lambda i, col: (0, 0)
+    return pl.pallas_call(
+        functools.partial(head_prep_kernel, n_ctx, nh),
+        grid_spec=pltpu.PrefetchScalarGridSpec(
+            num_scalar_prefetch=1,
+            grid=(rows // tile,),
+            in_specs=[pl.BlockSpec((tile, width), row)] * 3
+            + [pl.BlockSpec((tile, 1), row)] * 2
+            + [pl.BlockSpec((1, width), fixed)] * 2
+            + [pl.BlockSpec((tile, HD), row)] * 2,
+            out_specs=[pl.BlockSpec((3, tile, HD), lambda i, col: (0, i, 0))] * (n_ctx * nh),
+        ),
+        out_shape=[jax.ShapeDtypeStruct((3, rows, HD), BF16)] * (n_ctx * nh),
+        compiler_params=vmem(32),
+        cost_estimate=cost(12 * rows * width, 12 * rows * width),
+    )(col, q_raw, k_raw, value, q_scale, k_scale, q_gain, k_gain, cosine, sine)
+
+
+def back_sums_kernel(n_ctx, head, col_ref, *refs):
+    parts = refs[:n_ctx]
+    ins = refs[n_ctx : 3 * n_ctx]
+    qs_ref, ks_ref, qg_ref, kg_ref, cos_ref, sin_ref = refs[3 * n_ctx : -3]
+    sums_ref, qgain_ref, kgain_ref = refs[-3:]
+    cosine = cos_ref[...]
+    sine = sin_ref[...]
+    q_scale = qs_ref[...]
+    k_scale = ks_ref[...]
+
+    @pl.when(pl.program_id(0) == 0)
+    def _():
+        qgain_ref[...] = jnp.zeros_like(qgain_ref)
+        kgain_ref[...] = jnp.zeros_like(kgain_ref)
+
+    q_total = jnp.zeros_like(cosine)
+    k_total = jnp.zeros_like(cosine)
+    for s in range(n_ctx):
+        cols = col_slice(col_ref, s, head)
+        q_term = turned_back(parts[s][0].astype(F32), cosine, sine) * ins[2 * s][...]
+        q_total += q_term * qg_ref[:, cols]
+        qgain_ref[:, cols] += jnp.sum(q_term * q_scale, axis=0, keepdims=True)
+        k_term = turned_back(parts[s][1].astype(F32), cosine, sine) * ins[2 * s + 1][...]
+        k_total += k_term * kg_ref[:, cols]
+        kgain_ref[:, cols] += jnp.sum(k_term * k_scale, axis=0, keepdims=True)
+    sums_ref[0:1, :] = jnp.sum(q_total.T, axis=0, keepdims=True)
+    sums_ref[1:2, :] = jnp.sum(k_total.T, axis=0, keepdims=True)
+
+
+def back_sums(col, parts, q_raw, k_raw, q_scale, k_scale, q_gain, k_gain, cosine, sine, head):
+    n_ctx = len(parts)
+    rows, width = q_raw.shape
+    tile = min(256, rows)
+    row = lambda i, col: (i, 0)
+    fixed = lambda i, col: (0, 0)
+    in_specs = [pl.BlockSpec((2, tile, HD), lambda i, col: (0, i, 0)) for _ in parts]
+    operands = list(parts)
+    for s in range(n_ctx):
+        for raw in (q_raw, k_raw):
+            in_specs.append(pl.BlockSpec((tile, HD), lambda i, col, s=s: (i, col[s] // HD + head)))
+            operands.append(raw)
+    return pl.pallas_call(
+        functools.partial(back_sums_kernel, n_ctx, head),
+        grid_spec=pltpu.PrefetchScalarGridSpec(
+            num_scalar_prefetch=1,
+            grid=(rows // tile,),
+            in_specs=in_specs
+            + [pl.BlockSpec((tile, 1), row)] * 2
+            + [pl.BlockSpec((1, width), fixed)] * 2
+            + [pl.BlockSpec((tile, HD), row)] * 2,
+            out_specs=[pl.BlockSpec((2, tile), lambda i, col: (0, i))]
+            + [pl.BlockSpec((1, width), fixed)] * 2,
+        ),
+        out_shape=[jax.ShapeDtypeStruct((2, rows), F32)]
+        + [jax.ShapeDtypeStruct((1, width), F32)] * 2,
+        compiler_params=vmem(32),
+        cost_estimate=cost(20 * rows * n_ctx * HD, 12 * rows * n_ctx * HD, weight=20000),
+    )(col, *operands, q_scale, k_scale, q_gain, k_gain, cosine, sine)
+
+
+def back_prep_kernel(n_ctx, nh, col_ref, *refs):
+    parts = refs[: n_ctx * nh]
+    (q_ref, k_ref, qs_ref, ks_ref, qm_ref, km_ref, qg_ref, kg_ref, cos_ref, sin_ref) = refs[
+        n_ctx * nh : n_ctx * nh + 10
+    ]
+    qw_ref, kw_ref, vw_ref = refs[-5:-2]
+    d_ref, in_ref = refs[-2:]
+    cosine = cos_ref[...]
+    sine = sin_ref[...]
+    q_scale = qs_ref[...]
+    k_scale = ks_ref[...]
+    q_mean = qm_ref[...]
+    k_mean = km_ref[...]
+    for h in range(nh):
+        for s in range(n_ctx):
+            cols = col_slice(col_ref, s, h)
+            part = parts[h * n_ctx + s]
+            dq = turned_back(part[0].astype(F32), cosine, sine) * qg_ref[:, cols]
+            d_ref[0, :, cols] = (dq * q_scale - q_ref[:, cols] * q_mean).astype(BF16)
+            dk = turned_back(part[1].astype(F32), cosine, sine) * kg_ref[:, cols]
+            d_ref[1, :, cols] = (dk * k_scale - k_ref[:, cols] * k_mean).astype(BF16)
+            d_ref[2, :, cols] = part[2]
+    total = times_trans(d_ref[0], qw_ref[...])
+    total += times_trans(d_ref[1], kw_ref[...])
+    total += times_trans(d_ref[2], vw_ref[...])
+    in_ref[...] = total.astype(BF16)
+
+
+def back_prep(
+    c, count, col, parts, q_raw, k_raw, q_scale, k_scale, q_mean, k_mean, q_gain, k_gain, cosine, sine,
+    q_weight, k_weight, v_weight, n_ctx, nh
+):
+    width = q_raw.shape[1]
+    depth = q_weight.shape[0]
+    tile = min(256, count)
+    first = c * count // tile
+    row = lambda i, col: (first + i, 0)
+    here = lambda i, col: (i, 0)
+    fixed = lambda i, col: (0, 0)
+    return pl.pallas_call(
+        functools.partial(back_prep_kernel, n_ctx, nh),
+        grid_spec=pltpu.PrefetchScalarGridSpec(
+            num_scalar_prefetch=1,
+            grid=(count // tile,),
+            in_specs=[pl.BlockSpec((3, tile, HD), lambda i, col: (0, first + i, 0))] * (n_ctx * nh)
+            + [pl.BlockSpec((tile, width), row)] * 2
+            + [pl.BlockSpec((tile, 1), row)] * 4
+            + [pl.BlockSpec((1, width), fixed)] * 2
+            + [pl.BlockSpec((tile, HD), row)] * 2
+            + [pl.BlockSpec((depth, width), fixed)] * 3,
+            out_specs=[
+                pl.BlockSpec((3, tile, width), lambda i, col: (0, i, 0)),
+                pl.BlockSpec((tile, depth), here),
+            ],
+        ),
+        out_shape=[
+            jax.ShapeDtypeStruct((3, count, width), BF16),
+            jax.ShapeDtypeStruct((count, depth), BF16),
+        ],
+        compiler_params=vmem(56),
+        cost_estimate=cost(6 * count * width * depth, 6 * width * depth + 20 * count * width),
+    )(
+        col, *parts, q_raw, k_raw, q_scale, k_scale, q_mean, k_mean, q_gain, k_gain, cosine, sine,
+        q_weight, k_weight, v_weight,
+    )
+
+
+def causal(keys, queries, first):
+    key = lax.broadcasted_iota(jnp.int32, (keys, queries), 0) + first
+    query = lax.broadcasted_iota(jnp.int32, (keys, queries), 1)
+    return key <= query
+
+
+def by_eights(value):
+    return value.reshape(value.shape[0] // 8, 8, value.shape[1])
+
+
+def attend_kernel(n_ctx, per, block, sub, wide, place_ref, *refs):
+    qkvs = refs[:n_ctx]
+    outs = refs[n_ctx : 2 * n_ctx]
+    ot_ref, lse_ref, qt_s, k_s, vt_s, score_s = refs[2 * n_ctx :]
+    blocks = n_ctx * per
+    factor = HD ** (-0.5) * LOG2E
+
+    def spots(g):
+        there = pl.ds(pl.multiple_of(place_ref[g] * block, block), block)
+        return g // per, slice((g % per) * block, (g % per + 1) * block), there
+
+    for g in range(blocks):
+        r, here, there = spots(g)
+        qt_s[:, there] = qkvs[r][0, here, :].T
+        k_s[there, :] = qkvs[r][1, here, :]
+        vt_s[:, there] = qkvs[r][2, here, :].T
+
+    def query_step(i, _):
+        mine = pl.ds(pl.multiple_of(i * block, block), block)
+        qt = qt_s[:, mine]
+        last = i * block // wide
+
+        def part(j, u):
+            return pl.ds(pl.multiple_of(j * wide + u * sub, sub), sub)
+
+        def score_step(j, top, masked=False):
+            for u in range(wide // sub):
+                scores = plain(k_s[part(j, u), :], qt)
+                if masked:
+                    scores = jnp.where(
+                        causal(sub, block, j * wide + u * sub - i * block), scores, NEG
+                    )
+                score_s[part(j, u), :] = scores
+                top = jnp.maximum(top, jnp.max(by_eights(scores), axis=0))
+            return top
+
+        top = score_step(last, jnp.full((8, block), NEG, F32), masked=True)
+        top = lax.fori_loop(0, last, score_step, top)
+        top = jnp.max(top, axis=0, keepdims=True) * factor
+
+        def value_step(j, carry):
+            total, acc = carry
+            for u in range(wide // sub):
+                expo = jnp.exp2(score_s[part(j, u), :] * factor - top)
+                total = total + jnp.sum(by_eights(expo), axis=0)
+                acc = acc + plain(vt_s[:, part(j, u)], expo.astype(BF16))
+            return total, acc
+
+        start = (jnp.zeros((8, block), F32), jnp.zeros((HD, block), F32))
+        total, acc = lax.fori_loop(0, last + 1, value_step, start)
+        total = jnp.sum(total, axis=0, keepdims=True)
+        ot_ref[:, mine] = acc / total
+        lse_ref[:, mine] = top + jnp.log2(total)
+        return 0
+
+    lax.fori_loop(0, blocks, query_step, 0)
+    for g in range(blocks):
+        r, here, there = spots(g)
+        outs[r][here, :] = ot_ref[:, there].T.astype(BF16)
+
+
+def attend(place, qkvs, block):
+    n_ctx = len(qkvs)
+    rows = qkvs[0].shape[1]
+    per = rows // block
+    length = n_ctx * rows
+    whole = lambda: pl.BlockSpec(memory_space=pltpu.VMEM)
+    return pl.pallas_call(
+        functools.partial(attend_kernel, n_ctx, per, block, min(256, block), rows),
+        in_specs=[pl.BlockSpec(memory_space=pltpu.SMEM)] + [whole() for _ in qkvs],
+        out_specs=[whole() for _ in range(n_ctx + 2)],
+        out_shape=[jax.ShapeDtypeStruct((rows, HD), BF16)] * n_ctx
+        + [jax.ShapeDtypeStruct((HD, length), F32), jax.ShapeDtypeStruct((1, length), F32)],
+        scratch_shapes=[
+            pltpu.VMEM((HD, length), BF16),
+            pltpu.VMEM((length, HD), BF16),
+            pltpu.VMEM((HD, length), BF16),
+            pltpu.VMEM((length, block), F32),
+        ],
+        compiler_params=vmem(40),
+        cost_estimate=cost(6 * length * length * HD, 12 * length * HD, length * length // 2),
+    )(place, *qkvs)
+
+
+def attend_back_kernel(n_ctx, per, block, sub, wide, place_ref, *refs):
+    blocks = n_ctx * per
+    qkvs = refs[:n_ctx]
+    d_outs = refs[n_ctx : n_ctx + blocks]
+    rest = refs[n_ctx + blocks :]
+    ot_ref, lse_ref = rest[:2]
+    grads = rest[2 : 2 + n_ctx]
+    q_s, qt_s, k_s, kt_s, v_s, do_s, dot_s, delta_s, dqt_s, dk_s, dv_s = rest[2 + n_ctx :]
+    scale = HD ** (-0.5)
+    factor = scale * LOG2E
+
+    def spots(g):
+        there = pl.ds(pl.multiple_of(place_ref[g] * block, block), block)
+        return g // per, slice((g % per) * block, (g % per + 1) * block), there
+
+    for g in range(blocks):
+        r, here, there = spots(g)
+        queries = qkvs[r][0, here, :]
+        q_s[there, :] = queries
+        qt_s[:, there] = queries.T
+        keys = qkvs[r][1, here, :]
+        k_s[there, :] = keys
+        kt_s[:, there] = keys.T
+        v_s[there, :] = qkvs[r][2, here, :]
+        d_out = d_outs[g][...]
+        do_s[there, :] = d_out
+        turned = d_out.T
+        dot_s[:, there] = turned
+        delta_s[:, there] = jnp.sum(turned.astype(F32) * ot_ref[:, there], axis=0, keepdims=True)
+    dqt_s[...] = jnp.zeros_like(dqt_s)
+    subs = block // sub
+    tiles = blocks * block // wide
+
+    def key_step(j, _):
+        part = lambda u: pl.ds(pl.multiple_of(j * block + u * sub, sub), sub)
+        first = j * block // wide
+
+        def query_step(i, carry, masked=False):
+            theirs = pl.ds(pl.multiple_of(i * wide, wide), wide)
+            lse = lse_ref[:, theirs]
+            delta = delta_s[:, theirs]
+            dqt = dqt_s[:, theirs]
+            sums = []
+            for u in range(subs):
+                dk, dv = carry[u]
+                scores = plain(k_s[part(u), :], qt_s[:, theirs])
+                d_probs = plain(v_s[part(u), :], dot_s[:, theirs])
+                probs = jnp.exp2(scores * factor - lse)
+                if masked:
+                    probs = jnp.where(causal(sub, wide, j * block + u * sub - i * wide), probs, 0.0)
+                d_scores = (probs * (d_probs - delta)).astype(BF16)
+                dv = dv + plain(probs.astype(BF16), do_s[theirs, :])
+                dk = dk + plain(d_scores, q_s[theirs, :])
+                dqt = dqt + plain(kt_s[:, part(u)], d_scores)
+                sums.append((dk, dv))
+            dqt_s[:, theirs] = dqt
+            return tuple(sums)
+
+        zero = jnp.zeros((sub, HD), F32)
+        carry = query_step(first, ((zero, zero),) * subs, masked=True)
+        carry = lax.fori_loop(first + 1, tiles, query_step, carry)
+        for u in range(subs):
+            dk_s[part(u), :] = carry[u][0]
+            dv_s[part(u), :] = carry[u][1]
+        return 0
+
+    lax.fori_loop(0, blocks, key_step, 0)
+    for g in range(blocks):
+        r, here, there = spots(g)
+        out = grads[r]
+        out[0, here, :] = (dqt_s[:, there].T * scale).astype(BF16)
+        out[1, here, :] = (dk_s[there, :] * scale).astype(BF16)
+        out[2, here, :] = dv_s[there, :].astype(BF16)
+
+
+def attend_back(place, qkvs, d_outs, head, out_t, lse, block):
+    n_ctx = len(qkvs)
+    rows = qkvs[0].shape[1]
+    per = rows // block
+    length = n_ctx * rows
+    whole = lambda: pl.BlockSpec(memory_space=pltpu.VMEM)
+    return pl.pallas_call(
+        functools.partial(attend_back_kernel, n_ctx, per, block, min(256, block), block),
+        grid=(1,),
+        in_specs=[pl.BlockSpec(memory_space=pltpu.SMEM)]
+        + [whole() for _ in qkvs]
+        + [pl.BlockSpec((block, HD), lambda i: (0, head)) for _ in d_outs]
+        + [whole(), whole()],
+        out_specs=[whole() for _ in range(n_ctx)],
+        out_shape=[jax.ShapeDtypeStruct((3, rows, HD), BF16)] * n_ctx,
+        scratch_shapes=[
+            pltpu.VMEM((length, HD), BF16),
+            pltpu.VMEM((HD, length), BF16),
+            pltpu.VMEM((length, HD), BF16),
+            pltpu.VMEM((HD, length), BF16),
+            pltpu.VMEM((length, HD), BF16),
+            pltpu.VMEM((length, HD), BF16),
+            pltpu.VMEM((HD, length), BF16),
+            pltpu.VMEM((1, length), F32),
+            pltpu.VMEM((HD, length), F32),
+            pltpu.VMEM((length, HD), F32),
+            pltpu.VMEM((length, HD), F32),
+        ],
+        compiler_params=vmem(48),
+        cost_estimate=cost(8 * length * length * HD, 20 * length * HD, length * length // 2),
+    )(place, *qkvs, *d_outs, out_t, lse)
+
+
+def join_kernel(nh, per, block, col_ref, *refs):
+    n_parts = len(refs) - per
+    parts, outs = refs[:n_parts], refs[n_parts:]
+    for j, part in enumerate(parts):
+        cols = col_slice(col_ref, j // nh, j % nh)
+        for c in range(per):
+            outs[c][:, cols] = part[c * block : (c + 1) * block, :]
+
+
+def join_heads(col, parts, nh, per):
+    rows = parts[0].shape[0]
+    block = rows // per
+    width = len(parts) * HD
+    whole = lambda: pl.BlockSpec(memory_space=pltpu.VMEM)
+    return pl.pallas_call(
+        functools.partial(join_kernel, nh, per, block),
+        in_specs=[pl.BlockSpec(memory_space=pltpu.SMEM)] + [whole() for _ in parts],
+        out_specs=[whole() for _ in range(per)],
+        out_shape=[jax.ShapeDtypeStruct((block, width), BF16)] * per,
+        compiler_params=vmem(24),
+        cost_estimate=cost(0, 4 * rows * width),
+    )(col, *parts)
+
+
+def branch_kernel(count, me_ref, *refs):
+    atts, weights = refs[:count], refs[count : 2 * count]
+    x_ref, gain_ref, branch_ref, low_ref = refs[2 * count :]
+
+    def add_up(order):
+        branch = times_trans(atts[order[0]][...], weights[order[0]][...])
+        for i in order[1:]:
+            branch = branch + times_trans(atts[i][...], weights[i][...])
+        branch_ref[...] = branch
+        hidden = x_ref[...].astype(F32) + branch * rms(branch) * gain_ref[...]
+        low_ref[...] = hidden.astype(BF16)
+
+    if count == 2:
+        pl.when(me_ref[0] == 0)(lambda: add_up((0, 1)))
+        pl.when(me_ref[0] != 0)(lambda: add_up((1, 0)))
+    else:
+        add_up(range(count))
+
+
+def branch_rows(c, atts, weights, tokens, gain):
+    rows, wide = atts[0].shape
+    depth = weights[0].shape[0]
+    tile = min(256, rows)
+    first = c * rows // tile
+    fixed = lambda i: (0, 0)
+    here = lambda i: (i, 0)
+    return pl.pallas_call(
+        functools.partial(branch_kernel, len(atts)),
+        grid=(rows // tile,),
+        in_specs=[pl.BlockSpec(memory_space=pltpu.SMEM)]
+        + [pl.BlockSpec((tile, wide), here) for _ in atts]
+        + [pl.BlockSpec((depth, wide), fixed) for _ in weights]
+        + [pl.BlockSpec((tile, depth), lambda i: (first + i, 0)), pl.BlockSpec((1, depth), fixed)],
+        out_specs=[pl.BlockSpec((tile, depth), here)] * 2,
+        out_shape=[
+            jax.ShapeDtypeStruct((rows, depth), F32),
+            jax.ShapeDtypeStruct((rows, depth), BF16),
+        ],
+        compiler_params=vmem(48),
+        cost_estimate=cost(2 * rows * wide * depth * len(atts), 8 * rows * depth + 2 * depth * wide * len(atts)),
+    )(lax.axis_index("tensor").reshape(1).astype(jnp.int32), *atts, *weights, tokens, gain)
+
+
+def middle_kernel(count, *refs):
+    parts = refs[:count]
+    cot_ref, branch_ref, x_ref, again_ref, mgain_ref = refs[count : count + 5]
+    out_ref, dmixed_ref, gain_ref = refs[-3:]
+    mixed = parts[0][...].astype(F32)
+    for part in parts[1:]:
+        mixed = mixed + part[...].astype(F32)
+    branch = branch_ref[...]
+    hidden = x_ref[...].astype(F32) + branch * rms(branch) * again_ref[...]
+    scale = rms(mixed)
+    mgain = mgain_ref[...]
+    normed = mixed * scale
+    out_ref[...] = (hidden + normed * mgain).astype(BF16)
+    grad = cot_ref[...].astype(F32)
+
+    @pl.when(pl.program_id(0) == 0)
+    def _():
+        gain_ref[...] = jnp.zeros_like(gain_ref)
+
+    gain_ref[...] += jnp.sum(grad * normed, axis=0, keepdims=True)
+    weighted = grad * mgain
+    mean = jnp.mean(weighted * normed, axis=-1, keepdims=True)
+    dmixed_ref[...] = (scale * (weighted - normed * mean)).astype(BF16)
+
+
+def middle_rows(c, parts, cot, branch, tokens, attn_gain, mlp_gain, output):
+    rows, width = parts[0].shape
+    tile = min(128, rows)
+    first = c * rows // tile
+    here = lambda i: (i, 0)
+    there = lambda i: (first + i, 0)
+    fixed = lambda i: (0, 0)
+    return pl.pallas_call(
+        functools.partial(middle_kernel, len(parts)),
+        grid=(rows // tile,),
+        in_specs=[pl.BlockSpec((tile, width), here) for _ in parts]
+        + [
+            pl.BlockSpec((tile, width), there),
+            pl.BlockSpec((tile, width), here),
+            pl.BlockSpec((tile, width), there),
+            pl.BlockSpec((1, width), fixed),
+            pl.BlockSpec((1, width), fixed),
+        ]
+        + [pl.BlockSpec(memory_space=pl.ANY) for _ in output],
+        out_specs=[
+            pl.BlockSpec((tile, width), there),
+            pl.BlockSpec((tile, width), here),
+            pl.BlockSpec((1, width), fixed),
+        ],
+        out_shape=[
+            jax.ShapeDtypeStruct(tokens.shape, BF16),
+            jax.ShapeDtypeStruct((rows, width), BF16),
+            jax.ShapeDtypeStruct((1, width), F32),
+        ],
+        input_output_aliases={len(parts) + 5: 0} if output else {},
+        compiler_params=vmem(32),
+        cost_estimate=cost(30 * rows * width, 16 * rows * width),
+    )(*parts, cot, branch, tokens, attn_gain, mlp_gain, *output)
+
+
+def total_kernel(count, *refs):
+    total = refs[0][...].astype(F32)
+    for part in refs[1:count]:
+        total = total + part[...].astype(F32)
+    refs[-1][...] = total.astype(BF16)
+
+
+def total_rows(c, cot, parts, output):
+    rows, width = parts[0].shape
+    tile = min(128, rows)
+    first = c * rows // tile
+    there = lambda i: (first + i, 0)
+    return pl.pallas_call(
+        functools.partial(total_kernel, 1 + len(parts)),
+        grid=(rows // tile,),
+        in_specs=[pl.BlockSpec((tile, width), there)]
+        + [pl.BlockSpec((tile, width), lambda i: (i, 0)) for _ in parts]
+        + [pl.BlockSpec(memory_space=pl.ANY) for _ in output],
+        out_specs=pl.BlockSpec((tile, width), there),
+        out_shape=jax.ShapeDtypeStruct(cot.shape, BF16),
+        input_output_aliases={1 + len(parts): 0} if output else {},
+        compiler_params=vmem(32),
+        cost_estimate=cost(6 * rows * width, 12 * rows * width),
+    )(cot, *parts, *output)
+
+
+def last_kernel(count, *refs):
+    parts = refs[:count]
+    cot_ref, branch_ref, again_ref, dbranch_ref, gain_ref = refs[count:]
+    total = parts[0][...].astype(F32)
+    for part in parts[1:]:
+        total = total + part[...].astype(F32)
+    d_hidden = cot_ref[...].astype(F32) + total
+    branch = branch_ref[...]
+    scale = rms(branch)
+    normed = branch * scale
+
+    @pl.when(pl.program_id(0) == 0)
+    def _():
+        gain_ref[...] = jnp.zeros_like(gain_ref)
+
+    gain_ref[...] += jnp.sum(d_hidden * normed, axis=0, keepdims=True)
+    weighted = d_hidden * again_ref[...]
+    mean = jnp.mean(weighted * normed, axis=-1, keepdims=True)
+    dbranch_ref[...] = (scale * (weighted - normed * mean)).astype(BF16)
+
+
+def last_rows(c, parts, cot, branch, attn_gain):
+    rows, width = parts[0].shape
+    tile = min(128, rows)
+    first = c * rows // tile
+    here = lambda i: (i, 0)
+    there = lambda i: (first + i, 0)
+    fixed = lambda i: (0, 0)
+    return pl.pallas_call(
+        functools.partial(last_kernel, len(parts)),
+        grid=(rows // tile,),
+        in_specs=[pl.BlockSpec((tile, width), here) for _ in parts]
+        + [
+            pl.BlockSpec((tile, width), there),
+            pl.BlockSpec((tile, width), here),
+            pl.BlockSpec((1, width), fixed),
+        ],
+        out_specs=[pl.BlockSpec((tile, width), here), pl.BlockSpec((1, width), fixed)],
+        out_shape=[
+            jax.ShapeDtypeStruct((rows, width), BF16),
+            jax.ShapeDtypeStruct((1, width), F32),
+        ],
+        compiler_params=vmem(32),
+        cost_estimate=cost(20 * rows * width, 12 * rows * width, weight=LONG if c == 0 else 1),
+    )(*parts, cot, branch, attn_gain)
+
+
+def forward_kernel(sub, x_ref, gw_ref, uw_ref, dw_ref, slope_ref, silu_ref, inner_ref, mixed_ref, acc):
+    step = pl.program_id(0)
+    x = x_ref[...]
+    for t in range(gw_ref.shape[1] // sub):
+        span = slice(t * sub, (t + 1) * sub)
+        gate = plain(x, gw_ref[:, span])
+        up = plain(x, uw_ref[:, span])
+        sigmoid = 1.0 / (1.0 + jnp.exp2(gate * (-LOG2E)))
+        silu = gate * sigmoid
+        inner_ref[:, span] = (silu * up).astype(BF16)
+        silu_ref[:, span] = silu.astype(BF16)
+        slope_ref[:, span] = (up * (sigmoid + silu * (1.0 - sigmoid))).astype(BF16)
+    product = times_trans(inner_ref[...], dw_ref[...])
+
+    @pl.when(step == 0)
+    def _():
+        acc[...] = product
+
+    @pl.when(step > 0)
+    def _():
+        acc[...] += product
+
+    @pl.when(step == pl.num_programs(0) - 1)
+    def _():
+        mixed_ref[...] = acc[...].astype(BF16)
+
+
+def forward_rows(x, gate_weight, up_weight, down_weight):
+    rows, depth = x.shape
+    units = gate_weight.shape[1]
+    tile = min(512, units)
+    column = lambda i: (0, i)
+    fixed = lambda i: (0, 0)
+    return pl.pallas_call(
+        functools.partial(forward_kernel, min(256, tile)),
+        grid=(units // tile,),
+        in_specs=[pl.BlockSpec((rows, depth), fixed)] + [pl.BlockSpec((depth, tile), column)] * 3,
+        out_specs=[pl.BlockSpec((rows, tile), column)] * 3 + [pl.BlockSpec((rows, depth), fixed)],
+        out_shape=[jax.ShapeDtypeStruct((rows, units), BF16)] * 3
+        + [jax.ShapeDtypeStruct((rows, depth), BF16)],
+        scratch_shapes=[pltpu.VMEM((rows, depth), F32)],
+        compiler_params=vmem(48),
+        cost_estimate=cost(6 * rows * depth * units, 6 * depth * units + 6 * rows * units, rows * units),
+    )(x, gate_weight, up_weight, down_weight)
+
+
+def backward_kernel(sub, d_ref, dw_ref, gw_ref, uw_ref, slope_ref, silu_ref, both_ref, dhid_ref, acc):
+    step = pl.program_id(0)
+    d_mixed = d_ref[...]
+    for t in range(dw_ref.shape[1] // sub):
+        span = slice(t * sub, (t + 1) * sub)
+        d_inner = plain(d_mixed, dw_ref[:, span])
+        both_ref[0, :, span] = (d_inner * slope_ref[:, span].astype(F32)).astype(BF16)
+        both_ref[1, :, span] = (d_inner * silu_ref[:, span].astype(F32)).astype(BF16)
+    product = times_trans(both_ref[0], gw_ref[...]) + times_trans(both_ref[1], uw_ref[...])
+
+    @pl.when(step == 0)
+    def _():
+        acc[...] = product
+
+    @pl.when(step > 0)
+    def _():
+        acc[...] += product
+
+    @pl.when(step == pl.num_programs(0) - 1)
+    def _():
+        dhid_ref[...] = acc[...].astype(BF16)
+
+
+def backward_rows(d_mixed, down_weight, gate_weight, up_weight, slope, silu):
+    rows, depth = d_mixed.shape
+    units = gate_weight.shape[1]
+    tile = min(512, units)
+    column = lambda i: (0, i)
+    fixed = lambda i: (0, 0)
+    return pl.pallas_call(
+        functools.partial(backward_kernel, min(256, tile)),
+        grid=(units // tile,),
+        in_specs=[pl.BlockSpec((rows, depth), fixed)]
+        + [pl.BlockSpec((depth, tile), column)] * 3
+        + [pl.BlockSpec((rows, tile), column)] * 2,
+        out_specs=[pl.BlockSpec((2, rows, tile), lambda i: (0, 0, i)), pl.BlockSpec((rows, depth), fixed)],
+        out_shape=[
+            jax.ShapeDtypeStruct((2, rows, units), BF16),
+            jax.ShapeDtypeStruct((rows, depth), BF16),
+        ],
+        scratch_shapes=[pltpu.VMEM((rows, depth), F32)],
+        compiler_params=vmem(48),
+        cost_estimate=cost(6 * rows * depth * units, 6 * depth * units + 8 * rows * units),
+    )(d_mixed, down_weight, gate_weight, up_weight, slope, silu)
+
+
+def row_steps(first):
+    ctx_bits = [("ctx", 1 << i) for i in range(lax.axis_size("ctx").bit_length() - 1)]
+    dp_bits = [("dp", 1 << i) for i in range(lax.axis_size("dp").bit_length() - 1)]
+    if first == "ctx":
+        return ctx_bits + dp_bits
+    return ctx_bits[:1] + dp_bits + ctx_bits[1:]
+
+
+def row_order(steps):
+    dp = lax.axis_index("dp")
+    ctx = lax.axis_index("ctx")
+    order = []
+    for j in range(1 << len(steps)):
+        flips = {"dp": 0, "ctx": 0}
+        for place, (axis, bit) in enumerate(steps):
+            if j >> (len(steps) - 1 - place) & 1:
+                flips[axis] |= bit
+        order.append((dp ^ flips["dp"]) * lax.axis_size("ctx") + (ctx ^ flips["ctx"]))
+    return jnp.stack(order).astype(jnp.int32)
+
+
+def grad_kernel(pieces, chunks, piece, tokens, idx_ref, *refs):
+    lefts = refs[: pieces * chunks]
+    rights = refs[pieces * chunks : pieces * chunks + chunks]
+    outs, turned = refs[pieces * chunks + chunks : -1], refs[-1]
+
+    @pl.when(pl.program_id(0) == 0)
+    def _():
+        for p in range(pieces):
+            for c in range(chunks):
+                turned[p * piece : (p + 1) * piece, c * tokens : (c + 1) * tokens] = lefts[
+                    p * chunks + c
+                ][...].T
+
+    rows = pieces * piece
+    share = rows // len(outs)
+    step = min(256, rows)
+    for m in range(0, rows, step):
+        total = None
+        for c in range(chunks):
+            right = rights[c][0] if len(rights[c].shape) == 3 else rights[c][...]
+            term = plain(turned[m : m + step, c * tokens : (c + 1) * tokens], right)
+            total = term if total is None else total + term
+        total = total.astype(BF16)
+        size = min(share, step)
+        for i in range(m, m + step, size):
+            outs[i // share][i % share : i % share + size, :] = total[i - m : i - m + size]
+
+
+def grad_rows(index, lefts, rights, split):
+    pieces = index.shape[0]
+    chunks = len(lefts)
+    tokens = rights[0][0].shape[-2]
+    piece = lefts[0][0].shape[1] // (lax.axis_size("dp") * lax.axis_size("ctx"))
+    width = rights[0][0].shape[-1]
+    tile = min(512, width)
+    count = width // tile
+    rows = pieces * piece
+    in_specs = []
+    operands = []
+    for p in range(pieces):
+        for left, c in lefts:
+            in_specs.append(pl.BlockSpec((tokens, piece), lambda n, idx, p=p, c=c: (c, idx[p])))
+            operands.append(left)
+    for right, which in rights:
+        if which is None:
+            in_specs.append(pl.BlockSpec((tokens, tile), lambda n, idx: (0, n)))
+        else:
+            in_specs.append(pl.BlockSpec((1, tokens, tile), lambda n, idx, which=which: (which, 0, n)))
+        operands.append(right)
+    return pl.pallas_call(
+        functools.partial(grad_kernel, pieces, chunks, piece, tokens),
+        grid_spec=pltpu.PrefetchScalarGridSpec(
+            num_scalar_prefetch=1,
+            grid=(count,),
+            in_specs=in_specs,
+            out_specs=[pl.BlockSpec((rows // split, tile), lambda n, idx: (0, n))] * split,
+            scratch_shapes=[pltpu.VMEM((rows, chunks * tokens), BF16)],
+        ),
+        out_shape=[jax.ShapeDtypeStruct((rows // split, width), BF16)] * split,
+        compiler_params=vmem(40),
+        cost_estimate=cost(
+            2 * rows * tokens * chunks * width, 2 * (rows + tokens * chunks) * width + 2 * rows * width
+        ),
+    )(index, *operands)
+
+
+def near(value):
+    return swap(value, "ctx", 1)
+
+
+class Gradient:
+    def __init__(self, lefts, rights, steps, which=None):
+        self.steps = steps
+        self.lefts = [left if isinstance(left, tuple) else (left, 0) for left in lefts]
+        self.rights = [(right, which) for right in rights]
+        index = row_order(steps)
+        self.index = index[: index.shape[0] // 2]
+        self.place = 1
+
+    def multiply(self, *gates):
+        index = after(self.index, *gates)
+        self.low, self.high = grad_rows(index, self.lefts, self.rights, 2)
+        return self.low
+
+    def step(self, *gates):
+        came = swap(self.high, *self.steps[self.place])
+        if gates:
+            came = after(came, *gates)
+        self.place += 1
+        if self.place == len(self.steps):
+            self.low = self.low.astype(F32) + came.astype(F32)
+        else:
+            half = self.low.shape[0] // 2
+            self.high = (self.low[half:].astype(F32) + came[half:].astype(F32)).astype(BF16)
+            self.low = (self.low[:half].astype(F32) + came[:half].astype(F32)).astype(BF16)
+        return self.low
+
+    def result(self):
+        while self.place < len(self.steps):
+            self.step()
+        return self.low
+
+
+class PiecedGradient(Gradient):
+    def multiply(self, *gates):
+        index = after(self.index, *gates)
+        self.blocks = grad_rows(index, self.lefts, self.rights, index.shape[0])
+        self.came = {}
+        return self.blocks[0]
+
+    def send(self, i, *gates):
+        block = self.blocks[len(self.blocks) // 2 + i]
+        if gates:
+            block = after(block, *gates)
+        self.came[i] = swap(block, *self.steps[self.place])
+        return self.came[i]
+
+    def add(self, *gates):
+        half = len(self.blocks) // 2
+        for i in range(half):
+            if i not in self.came:
+                self.send(i)
+        kind = F32 if half == 1 else BF16
+        self.blocks = [
+            (self.blocks[i].astype(F32) + after(self.came[i], *gates).astype(F32)).astype(kind)
+            for i in range(half)
+        ]
+        self.came = {}
+        self.place += 1
+        return self.blocks[0]
+
+    def result(self):
+        while len(self.blocks) > 1:
+            self.add()
+        return self.blocks[0]
+
+
+def on_device(
+    tokens,
+    q_weight,
+    k_weight,
+    v_weight,
+    o_weight,
+    gate_weight,
+    up_weight,
+    down_weight,
+    q_gain,
+    k_gain,
+    attn_gain,
+    mlp_gain,
+    group_order,
+    cotangent,
+):
+    local, seqs, width = tokens.shape
+    rows = local * seqs
+    n_ctx = lax.axis_size("ctx")
+    me = lax.axis_index("ctx")
+    heads_here = q_weight.shape[1] // HD
+    nh = heads_here // n_ctx
+    features = H * HD
+    groups = group_order.shape[1]
+    length = local * n_ctx
+    block = length // groups
+    per = local // block
+    flat = tokens.reshape(rows, width)
+    cot = cotangent.reshape(rows, width)
+    again = attn_gain.reshape(1, -1)
+    mgain = mlp_gain.reshape(1, -1)
+
+    others = [me ^ s for s in range(n_ctx)]
+    rel = jnp.stack(others).astype(jnp.int32)
+    col = rel * (nh * HD)
+    order = group_order.reshape(groups)
+    place = jnp.concatenate(
+        [lax.dynamic_slice_in_dim(order, o * per, per, 0) for o in others]
+    ).astype(jnp.int32)
+
+    y_first = row_steps("ctx")
+    z_first = row_steps("dp")
+
+    query_raw, key_raw, sums = qk_project(flat, q_weight, k_weight)
+    value = plain(after(flat, sums), v_weight).astype(BF16)
+    scales = lax.rsqrt(tensor_sum(sums) / features + EPS)
+    q_scale = scales[0][:, None]
+    k_scale = scales[1][:, None]
+    own_order = lax.dynamic_slice_in_dim(order, me * per, per, 0)
+    query_pos = (own_order[:, None] * block + jnp.arange(block, dtype=jnp.int32)[None, :]).reshape(local)
+    freq = jnp.power(THETA, -jnp.arange(HD // 2, dtype=F32) * 2.0 / HD)
+    angle = query_pos.astype(F32)[:, None] * freq
+    cosine = jnp.cos(angle)
+    sine = jnp.sin(angle)
+    cosine = jnp.concatenate([cosine, cosine], axis=1)
+    sine = jnp.concatenate([-sine, sine], axis=1)
+    qg = q_gain.reshape(1, -1)
+    kg = k_gain.reshape(1, -1)
+    packed = head_prep(col, query_raw, key_raw, value, q_scale, k_scale, qg, kg, cosine, sine, n_ctx, nh)
+    qkvs = []
+    for h in range(nh):
+        mine = packed[h * n_ctx : (h + 1) * n_ctx]
+        qkvs.append([mine[0]] + [swap(mine[s], "ctx", s) for s in range(1, n_ctx)])
+
+    o_weights = tensor_all(after(o_weight, packed[0]))
+
+    attended = []
+    returned = []
+    for h in range(nh):
+        result = attend(place, qkvs[h], block)
+        attended.append(result[n_ctx:])
+        returned.append([result[0]] + [swap(result[s], "ctx", s) for s in range(1, n_ctx)])
+    att = join_heads(col, [returned[h][s] for s in range(n_ctx) for h in range(nh)], nh, per)
+
+    chunks = range(per)
+    with_near = lambda values: list(values) + [near(v) for v in values]
+    branch, lowered, slope, silu, inner, mixed = [], [], [], [], [], []
+    gate = None
+    for c in chunks:
+        b, low = branch_rows(c, tensor_all(att[c]), o_weights, flat, again)
+        branch.append(b)
+        lowered.append(low)
+        if gate is not None:
+            low = after(low, gate)
+        a, s, i, m = forward_rows(low, gate_weight, up_weight, down_weight)
+        gate = m
+        slope.append(a)
+        silu.append(s)
+        inner.append(i)
+        mixed.append(tensor_list(m))
+    output, d_mixed, mlp_terms, d_both, hid = [], [], [], [], []
+    d_branch, attn_terms, d_outs = [], [], []
+
+    def last(c, *gates):
+        hid[c][0] = after(hid[c][0], *gates)
+        d, term = last_rows(c, hid[c], cot, branch[c], again)
+        d_branch.append(d)
+        attn_terms.append(term)
+        pieces = project_pieces(col, d, o_weight, LONG if c == 0 else 1)
+        d_outs.append([pieces[0]] + [swap(pieces[s], "ctx", s) for s in range(1, n_ctx)])
+        return pieces[0]
+
+    for c in chunks:
+        if c:
+            mixed[c][0] = after(mixed[c][0], gate)
+        out, d, term = middle_rows(c, mixed[c], cot, branch[c], flat, again, mgain, output)
+        output = [out]
+        d_mixed.append(d)
+        mlp_terms.append(term)
+        if c == per - 1:
+            down_grad = PiecedGradient(with_near(d_mixed), with_near(inner), y_first)
+            d = after(d, down_grad.multiply())
+        g, h = backward_rows(d, down_weight, gate_weight, up_weight, slope[c], silu[c])
+        gate = h
+        d_both.append(g)
+        hid.append(tensor_list(h))
+    for c in range(per - 1):
+        gate = last(c, gate)
+    low_all, both_all = with_near(lowered), with_near(d_both)
+    gate_grad = PiecedGradient(low_all, both_all, z_first, 0)
+    gate = gate_grad.multiply(gate, down_grad.send(0))
+    up_grad = PiecedGradient(low_all, both_all, y_first, 1)
+    gate = up_grad.multiply(gate, down_grad.send(1))
+    gate = last(per - 1, gate, down_grad.send(2), gate_grad.send(0))
+    o_grad = Gradient(with_near(d_branch), with_near(att), z_first)
+    gate = o_grad.multiply(gate)
+    gates = [gate, gate_grad.send(1), down_grad.add(gate)]
+
+    parts, sums, q_terms, k_terms = [], [], [], []
+    for h in range(nh):
+        grads_in = [d_outs[c][s] for s in range(n_ctx) for c in chunks]
+        grads_in[0] = after(grads_in[0], *gates)
+        back = attend_back(place, qkvs[h], grads_in, h, attended[h][0], attended[h][1], block)
+        gates = [back[0]]
+        if h == 0:
+            arrived = [p for s, p in enumerate(d_outs[-1]) if s]
+            gates += [up_grad.send(0, *arrived), up_grad.send(1, *arrived), gate_grad.send(2)]
+        parts.append([back[0]] + [swap(back[s], "ctx", s) for s in range(1, n_ctx)])
+    gates += [down_grad.send(0), down_grad.send(1), gate_grad.send(3)]
+    for h in range(nh):
+        mine = [after(parts[h][0], *gates)] + parts[h][1:]
+        sum_h, q_term, k_term = back_sums(
+            col, mine, query_raw, key_raw, q_scale, k_scale, qg, kg, cosine, sine, h
+        )
+        gates = [sum_h]
+        sums.append(sum_h)
+        q_terms.append(q_term)
+        k_terms.append(k_term)
+    gate_grad.add(sums[0])
+    down_grad.add(sums[0])
+    o_grad.step(sums[0])
+    flat_parts = [part for mine in parts for part in mine]
+    both = tensor_sum(sum(sums)) / features
+    q_mean = both[0][:, None] * q_scale**3
+    k_mean = both[1][:, None] * k_scale**3
+    d_qkv, input_sums = [], []
+    for c in chunks:
+        d, part = back_prep(
+            c, block, col, flat_parts, query_raw, key_raw, q_scale, k_scale, after(q_mean, *gates), k_mean,
+            qg, kg, cosine, sine, q_weight, k_weight, v_weight, n_ctx, nh
+        )
+        gates = [part]
+        d_qkv.append(d)
+        input_sums.append(tensor_list(part))
+    flat_near = near(flat)
+    token_rows = [(t, c) for t in (flat, flat_near) for c in chunks]
+    qkv_all = with_near(d_qkv)
+    smalls = [Gradient(token_rows, qkv_all, y_first, i) for i in (2, 0, 1)]
+    gates += [up_grad.send(2), up_grad.send(3)]
+    for small in smalls:
+        gates = [small.multiply(*gates)]
+    up_grad.add(*gates)
+    o_grad.step(*gates)
+    done = [small.step(*gates) for small in smalls]
+    done += [down_grad.add(*done), gate_grad.add(*done)]
+
+    input_grad = []
+    for c in chunks:
+        terms = hid[c] + input_sums[c]
+        terms[0] = after(terms[0], *gates)
+        input_grad = [total_rows(c, cot, terms, input_grad)]
+
+    results = [small.result() for small in smalls]
+    gains = jnp.concatenate([sum(q_terms), sum(k_terms), sum(attn_terms), sum(mlp_terms)], axis=1)
+    gains = after(gains.reshape(-1, 128), *gates, *done, input_grad[0])
+    for axis, bit in y_first:
+        gains = gains + swap(gains, axis, bit)
+    gains = gains.reshape(-1)
+    own = heads_here * HD
+
+    return (
+        output[0].reshape(local, seqs, width),
+        input_grad[0].reshape(local, seqs, width),
+        results[1],
+        results[2],
+        results[0],
+        o_grad.result(),
+        gate_grad.result(),
+        up_grad.result(),
+        down_grad.result(),
+        gains[:own],
+        gains[own : 2 * own],
+        gains[2 * own : 2 * own + width],
+        gains[2 * own + width :],
     )
 
 
@@ -66,7 +1228,7 @@
     return (attn_term, mlp_term)
 
 
-def on_device(
+def gathered_device(
     tokens,
     q_weight,
     k_weight,
@@ -317,6 +1479,8 @@
         P(),
         P(),
     )
+    heads_here = H // mesh.shape["tensor"]
+    whole_heads = heads_here % mesh.shape["ctx"] == 0
     return jax.shard_map(
-        on_device, mesh=mesh, in_specs=in_specs, out_specs=out_specs, check_vma=False
-    )
+        on_device if whole_heads else gathered_device, mesh=mesh, in_specs=in_specs, out_specs=out_specs, check_vma=False
+    )

time: 2110 us -> 1140 us (0.54)
  waiting for transfers between devices: 1110 us -> 392 us
  matrix products: 653 us -> 9.28 us
  Pallas kernels: 0 us -> 531 us
  other arithmetic: 166 us -> 47.6 us
  blocking collectives: 71 us -> 0 us
  starting transfers between devices: 0.84 us -> 69.3 us
    dot_general x27 -> x1, matrix products: 653 us -> 9.28 us  [plain(): return jnp.dot(left, right, preferred_element_type=F32)]
    pallas_call x0 -> x32, Pallas kernels: none -> 531 us  [the longest x7 120 us: grad_rows(): pl.pallas_call(functools.partial(grad_kernel, pieces, chunks, piece, toke...]
    reduce_scatter x5 -> x0, waiting for transfers between devices: 491 us -> none  [the longest x1 180 us: on_device(): lax.psum_scatter(up_grad.astype(jnp.bfloat16), ('dp', 'ctx'), scatter_dim...]
    ppermute x0 -> x87, waiting for transfers between devices: none -> 392 us  [swap(): return lax.ppermute(value, axis, [(i, i ^ step) for i in range(count)])]
    psum x4 -> x0, waiting for transfers between devices: 371 us -> none  [branch_total(): lax.psum(term(0, total_rows).astype(jnp.bfloat16), 'tensor')]
    unnamed x17 -> x0, waiting for transfers between devices: 213 us -> none
    reduce_sum x9 -> x0, other arithmetic: 73.2 us -> none  [the longest x1 46.6 us: on_device(): total = jnp.sum(expo, axis=-1)]
    psum x3 -> x0, blocking collectives: 71 us -> none  [the longest x1 59.9 us: on_device(): lax.psum((q_gain_term, k_gain_term, attn_gain_part, mlp_gain_part), ('dp'...]
  transfers between devices with their start and end apart: 14 -> 87, of which waited for: 12 -> 30; matrix products, arithmetic and copies ran while one was open for 18% -> 5% of each run, Pallas kernels for 0% -> 44%
where the time goes in v1:
time: 1140 us; the launch traced here: 1130 us
  Pallas kernels  531 us (47%)
  waiting for transfers between devices  392 us (34%)
  local copies, waits for them, and re-layouts  79.6 us (7%)
  starting transfers between devices  69.3 us (6%)
  other arithmetic  47.6 us (4%)
    ppermute x87, waiting for transfers between devices, swap(): return lax.ppermute(value, axis, [(i, i ^ step) for i in range(count)])  392 us
    pallas_call x7, Pallas kernels, grad_rows(): pl.pallas_call(functools.partial(grad_kernel, pieces, chunks, piece, toke...  120 us
    unnamed x301, local copies, waits for them, and re-layouts  74.6 us
    pallas_call x2, Pallas kernels, backward_rows(): pl.pallas_call(functools.partial(backward_kernel, min(256, tile)), grid=(...  74.4 us
    pallas_call x2, Pallas kernels, forward_rows(): pl.pallas_call(functools.partial(forward_kernel, min(256, tile)), grid=(u...  74.2 us
    pallas_call x2, Pallas kernels, attend_back(): pl.pallas_call(functools.partial(attend_back_kernel, n_ctx, per, block, m...  72.7 us
    ppermute x87, starting transfers between devices, swap(): return lax.ppermute(value, axis, [(i, i ^ step) for i in range(count)])  69.3 us
    pallas_call x2, Pallas kernels, attend(): pl.pallas_call(functools.partial(attend_kernel, n_ctx, per, block, min(25...  46 us
  transfers between devices with their start and end apart: 87, of which 30 were waited for; matrix products, arithmetic and copies ran while one was open for 5% of the time, Pallas kernels for 44%

profile of v1, /device:TPU:0, one launch (start us, length us, event | category | flops | bytes accessed | tf_op | source)
XLA Modules:
  0.0 1130.9 jit_solution(8396889488932541346)
XLA Ops:
  5.0 22.9 %shard_map.237 = (f32[1024,1024]{1,0:T(8,128)S(1)}, f32[1024,1024]{1,0:T(8,128)S(1)}, f32[2,1024]{1,0:T(2,128)S(1)}) custom-call(bf16[1024,2048]{1,0:T(8,128)(2,1)} %bitcast.9.x_ref.refs_4_.refs_0_.refs_1_.refs_5_.refs_8_.refs_9_.refs_12_.refs_13_.refs_16_.refs_17_.refs_20_.refs_21_.refs_24_.refs_25_.refs_28_.refs_29_, bf16[2048,1024]{1,0:T(8,128)(2,1)S(1)} %copy-done.12, ...), custom_call_target="tpu_custom_call" | custom-call | flops 134217728 | bytes 327680 | tf_op jit(solution)/shard_map/pallas_call | solution.py:153
  64.3 16.1 %collective-permute-done.5.refs_2_ = bf16[3,1024,128]{2,1,0:T(8,128)(2,1)S(1)} collective-permute-done((bf16[3,1024,128]{2,1,0:T(8,128)(2,1)S(1)}, bf16[3,1024,128]{2,1,0:T(8,128)(2,1)S(1)}, u32[]{:S(2)}, u32[]{:S(2)}) %collective-permute-start.5) | collective-permute-done | bytes 786464 | tf_op jit(solution)/shard_map/ppermute | solution.py:38
  81.6 15.4 %collective-permute-done.6.refs_3_ = bf16[3,1024,128]{2,1,0:T(8,128)(2,1)} collective-permute-done((bf16[3,1024,128]{2,1,0:T(8,128)(2,1)}, bf16[3,1024,128]{2,1,0:T(8,128)(2,1)}, u32[]{:S(2)}, u32[]{:S(2)}) %collective-permute-start.6) | collective-permute-done | bytes 786464 | tf_op jit(solution)/shard_map/ppermute | solution.py:38
  97.0 22.9 %shard_map.240 = (bf16[1024,128]{1,0:T(8,128)(2,1)S(1)}, bf16[1024,128]{1,0:T(8,128)(2,1)S(1)}, bf16[1024,128]{1,0:T(8,128)(2,1)S(1)}, bf16[1024,128]{1,0:T(8,12...) custom-call(s32[8]{0:T(128)S(1)} %pad_add_fusion.place_ref, ...), custom_call_target="tpu_custom_call" | custom-call | flops 201326592 | bytes 98304 | tf_op jit(solution)/shard_map/pallas_call | solution.py:410
  130.7 23.2 %shard_map.239 = (bf16[1024,128]{1,0:T(8,128)(2,1)S(1)}, bf16[1024,128]{1,0:T(8,128)(2,1)S(1)}, bf16[1024,128]{1,0:T(8,128)(2,1)S(1)}, bf16[1024,128]{1,0:T(8,12...) custom-call(s32[8]{0:T(128)S(1)} %pad_add_fusion.place_ref, bf16[3,1024,128]{2,1,0:T(8,128)(2,1)S(1)} %copy-done.47, ...), custom_call_target="tpu_custom_call" | custom-call | flops 201326592 | bytes 98304 | tf_op jit(solution)/shard_map/pallas_call | solution.py:410
  172.7 24.0 %collective-permute-done.15.refs_1_ = bf16[512,1024]{1,0:T(8,128)(2,1)S(1)} collective-permute-done((bf16[512,1024]{1,0:T(8,128)(2,1)S(1)}, bf16[512,1024]{1,0:T(8,128)(2,1)S(1)}, u32[]{:S(2)}, u32[]{:S(2)}) %collective-permute-start.15) | collective-permute-done | bytes 1048608 | tf_op jit(solution)/shard_map/ppermute | solution.py:38
  209.6 36.2 %shard_map.244 = (bf16[512,4096]{1,0:T(8,128)(2,1)}, bf16[512,4096]{1,0:T(8,128)(2,1)}, bf16[512,4096]{1,0:T(8,128)(2,1)}, bf16[512,2048]{1,0:T(8,128)(2,1)S(1)}) custom-call(bf16[512,2048]{1,0:T(8,128)(2,1)S(1)} %get-tuple-element.192.x_ref.refs_0_.refs_4_.refs_8_.refs_12_.refs_16_.refs_20_.refs_24_.refs_28_, bf16[2048,4096]{1,0:T(8,128)(2,1)} %gw_ref.7, ...), custom_call_target="tpu_custom_call" | custom-call | flops 402653184 | bytes 983040 | tf_op jit(solution)/shard_map/pallas_call | solution.py:768
  258.7 38.0 %shard_map.245 = (bf16[512,4096]{1,0:T(8,128)(2,1)}, bf16[512,4096]{1,0:T(8,128)(2,1)}, bf16[512,4096]{1,0:T(8,128)(2,1)}, bf16[512,2048]{1,0:T(8,128)(2,1)}) custom-call(bf16[512,2048]{1,0:T(8,128)(2,1)S(1)} %get-tuple-element.194.x_ref.refs_1_.refs_5_.refs_9_.refs_13_.refs_17_.refs_21_.refs_25_.refs_29_, bf16[2048,4096]{1,0:T(8,128)(2,1)} %gw_ref.7, ...), custom_call_target="tpu_custom_call" | custom-call | flops 402653184 | bytes 983040 | tf_op jit(solution)/shard_map/pallas_call | solution.py:768
  312.0 37.1 %shard_map.247 = (bf16[2,512,4096]{2,1,0:T(8,128)(2,1)}, bf16[512,2048]{1,0:T(8,128)(2,1)S(1)}) custom-call(bf16[512,2048]{1,0:T(8,128)(2,1)} %get-tuple-element.197.d_ref.refs_0_.refs_4_.refs_8_.refs_12_.refs_16_.refs_20_.refs_24_.refs_28_, bf16[2048,4096]{1,0:T(8,128)(2,1)} %dw_ref.7, bf16[2048,4096]{1,0:T(8,128)(2,1)} %gw_ref.7, ...), custom_call_target="tpu_custom_call" | custom-call | flops 402653184 | bytes 1048576 | tf_op jit(solution)/shard_map/pallas_call | solution.py:810
  368.0 27.2 %shard_map.249 = (bf16[128,4096]{1,0:T(8,128)(2,1)S(1)}, bf16[128,4096]{1,0:T(8,128)(2,1)S(1)}, bf16[128,4096]{1,0:T(8,128)(2,1)S(1)}, bf16[128,4096]{1,0:T(8,12...) custom-call(s32[8]{0:T(128)S(1)} %stack.43.idx_ref, ...), custom_call_target="tpu_custom_call" | custom-call | flops 268435456 | bytes 524288 | tf_op jit(solution)/shard_map/pallas_call | solution.py:897
  401.1 37.3 %shard_map.250 = (bf16[2,512,4096]{2,1,0:T(8,128)(2,1)}, bf16[512,2048]{1,0:T(8,128)(2,1)S(1)}) custom-call(bf16[512,2048]{1,0:T(8,128)(2,1)} %get-tuple-element.209.refs_1_.refs_5_.refs_9_.refs_13_.refs_17_.refs_21_.refs_25_.refs_29_.d_ref, bf16[2048,4096]{1,0:T(8,128)(2,1)} %dw_ref.7, bf16[2048,4096]{1,0:T(8,128)(2,1)} %gw_ref.7, ...), custom_call_target="tpu_custom_call" | custom-call | flops 402653184 | bytes 1048576 | tf_op jit(solution)/shard_map/pallas_call | solution.py:810
  475.9 26.4 %shard_map.253 = (bf16[128,4096]{1,0:T(8,128)(2,1)S(1)}, bf16[128,4096]{1,0:T(8,128)(2,1)S(1)}, bf16[128,4096]{1,0:T(8,128)(2,1)S(1)}, bf16[128,4096]{1,0:T(8,12...) custom-call(s32[8]{0:T(128)S(1)} %stack.44.idx_ref, ...), custom_call_target="tpu_custom_call" | custom-call | flops 268435456 | bytes 524288 | tf_op jit(solution)/shard_map/pallas_call | solution.py:897
  511.9 27.0 %shard_map.254 = (bf16[128,4096]{1,0:T(8,128)(2,1)S(1)}, bf16[128,4096]{1,0:T(8,128)(2,1)S(1)}, bf16[128,4096]{1,0:T(8,128)(2,1)S(1)}, bf16[128,4096]{1,0:T(8,12...) custom-call(s32[8]{0:T(128)S(1)} %stack.43.idx_ref, ...), custom_call_target="tpu_custom_call" | custom-call | flops 268435456 | bytes 524288 | tf_op jit(solution)/shard_map/pallas_call | solution.py:897
  623.7 37.1 %shard_map.258 = (bf16[3,1024,128]{2,1,0:T(8,128)(2,1)S(1)}, bf16[3,1024,128]{2,1,0:T(8,128)(2,1)}, bf16[3,1024,128]{2,1,0:T(8,128)(2,1)}, bf16[3,1024,128]{2,1,0:T(8,128)(2,1)}) custom-call(s32[8]{0:T(128)S(1)} %copy-done.112, bf16[3,1024,128]{2,1,0:T(8,128)(2,1)S(1)} %copy-done.48, bf16[3,1024,128]{2,1,0:T(8,128)(2,1)} %collective-permute-done.1.refs_1_, ...), custom_call_target="tpu_custom_call" | custom-call | flops 268435456 | bytes 163840 | tf_op jit(solution)/shard_map/pallas_call | solution.py:508
  672.3 35.6 %shard_map.259 = (bf16[3,1024,128]{2,1,0:T(8,128)(2,1)S(1)}, bf16[3,1024,128]{2,1,0:T(8,128)(2,1)S(1)}, bf16[3,1024,128]{2,1,0:T(8,128)(2,1)S(1)}, bf16[3,1024,128]{2,1,0:T(8,128)(2,1)S(1)}) custom-call(s32[8]{0:T(128)S(1)} %copy-done.112, bf16[3,1024,128]{2,1,0:T(8,128)(2,1)S(1)} %copy-done.43, bf16[3,1024,128]{2,1,0:T(8,128)(2,1)} %copy-done.44, ...), custom_call_target="tpu_custom_call" | custom-call | flops 268435456 | bytes 163840 | tf_op jit(solution)/shard_map/pallas_call | solution.py:508
  763.3 17.7 %shard_map.262 = (bf16[3,512,1024]{2,1,0:T(8,128)(2,1)}, bf16[512,2048]{1,0:T(8,128)(2,1)}) custom-call(s32[4]{0:T(128)} %copy-done.110, bf16[3,1024,128]{2,1,0:T(8,128)(2,1)} %copy-done.35, bf16[3,1024,128]{2,1,0:T(8,128)(2,1)} %collective-permute-done.43.refs_1_, bf16[3,1024,128]{2,1,0:T(8,128)(2,1)} %collective-permute-done.44.refs_2_, ...), custom_call_target="tpu_custom_call" | custom-call | flops 100663296 | bytes 360448 | tf_op jit(solution)/shard_map/pallas_call | solution.py:305
  781.0 18.2 %shard_map.263 = (bf16[3,512,1024]{2,1,0:T(8,128)(2,1)}, bf16[512,2048]{1,0:T(8,128)(2,1)}) custom-call(s32[4]{0:T(128)} %copy-done.110, bf16[3,1024,128]{2,1,0:T(8,128)(2,1)} %copy-done.35, bf16[3,1024,128]{2,1,0:T(8,128)(2,1)} %collective-permute-done.43.refs_1_, bf16[3,1024,128]{2,1,0:T(8,128)(2,1)} %collective-permute-done.44.refs_2_, ...), custom_call_target="tpu_custom_call" | custom-call | flops 100663296 | bytes 360448 | tf_op jit(solution)/shard_map/pallas_call | solution.py:305
  811.7 17.4 %collective-permute-done.58 = bf16[128,4096]{1,0:T(8,128)(2,1)S(1)} collective-permute-done((bf16[128,4096]{1,0:T(8,128)(2,1)S(1)}, bf16[128,4096]{1,0:T(8,128)(2,1)S(1)}, u32[]{:S(2)}, u32[]{:S(2)}) %collective-permute-start.58) | collective-permute-done | bytes 1048608 | tf_op jit(solution)/shard_map/ppermute | solution.py:38
  877.9 22.3 %collective-permute-done.62.refs_4_ = bf16[512,2048]{1,0:T(8,128)(2,1)S(1)} collective-permute-done((bf16[512,2048]{1,0:T(8,128)(2,1)S(1)}, bf16[512,2048]{1,0:T(8,128)(2,1)S(1)}, u32[]{:S(2)}, u32[]{:S(2)}) %collective-permute-start.62) | collective-permute-done | bytes 2097184 | tf_op jit(solution)/shard_map/ppermute | solution.py:38
  907.5 22.1 %collective-permute-done.75 = bf16[128,1024]{1,0:T(8,128)(2,1)S(1)} collective-permute-done((bf16[128,1024]{1,0:T(8,128)(2,1)S(1)}, bf16[128,1024]{1,0:T(8,128)(2,1)S(1)}, u32[]{:S(2)}, u32[]{:S(2)}) %collective-permute-start.75) | collective-permute-done | bytes 262176 | tf_op jit(solution)/shard_map/ppermute | solution.py:38
  938.8 76.3 %collective-permute-done.77 = bf16[128,4096]{1,0:T(8,128)(2,1)S(1)} collective-permute-done((bf16[128,4096]{1,0:T(8,128)(2,1)S(1)}, bf16[128,4096]{1,0:T(8,128)(2,1)S(1)}, u32[]{:S(2)}, u32[]{:S(2)}) %collective-permute-start.77) | collective-permute-done | bytes 1048608 | tf_op jit(solution)/shard_map/ppermute | solution.py:38
  1021.5 26.1 %collective-permute-done.80 = bf16[128,4096]{1,0:T(8,128)(2,1)S(1)} collective-permute-done((bf16[128,4096]{1,0:T(8,128)(2,1)S(1)}, bf16[128,4096]{1,0:T(8,128)(2,1)S(1)}, u32[]{:S(2)}, u32[]{:S(2)}) %collective-permute-start.80) | collective-permute-done | bytes 1048608 | tf_op jit(solution)/shard_map/ppermute | solution.py:38
  1051.4 17.8 %collective-permute-done.71 = bf16[256,1024]{1,0:T(8,128)(2,1)S(1)} collective-permute-done((bf16[256,1024]{1,0:T(8,128)(2,1)S(1)}, bf16[256,1024]{1,0:T(8,128)(2,1)S(1)}, u32[]{:S(2)}, u32[]{:S(2)}) %collective-permute-start.71) | collective-permute-done | bytes 524320 | tf_op jit(solution)/shard_map/ppermute | solution.py:38
  1092.0 23.9 %collective-permute-done.72 = bf16[128,1024]{1,0:T(8,128)(2,1)S(1)} collective-permute-done((bf16[128,1024]{1,0:T(8,128)(2,1)S(1)}, bf16[128,1024]{1,0:T(8,128)(2,1)S(1)}, u32[]{:S(2)}, u32[]{:S(2)}) %collective-permute-start.72) | collective-permute-done | bytes 262176 | tf_op jit(solution)/shard_map/ppermute | solution.py:38
  (543 shorter events, 460.4 us)
Async XLA Ops:
  60.0 137.7 %collective-permute-start.14 = (bf16[2048,1024]{1,0:T(8,128)(2,1)}, bf16[2048,1024]{1,0:T(8,128)(2,1)}, u32[]{:S(2)}, u32[]{:S(2)}) collective-permute-start(bf16[2048,1024]{1,0:T(8,128)(2,1)} %w_ref.3), channel_id=1, source_target_pairs={{0,1},{1,0},{2,3},{3,2},{4,5},{5,4},{6,7},{7,6},{8,9},{9,8},{10,11... | collective-permute-start | bytes 12582920 | tf_op jit(solution)/shard_map/ppermute | solution.py:38
  172.2 75.2 %collective-permute-start.13 = (bf16[512,1024]{1,0:T(8,128)(2,1)}, bf16[512,1024]{1,0:T(8,128)(2,1)}, u32[]{:S(2)}, u32[]{:S(2)}) collective-permute-start(bf16[512,1024]{1,0:T(8,128)(2,1)} %get-tuple-element.188.refs_0_.refs_33_), channel_id=1, source_target_pairs={{0,1},{1,0},{2,3},{3,2},{4,5},{5,4},{6,7},{7,6},{8,9},{9,8},{10,11... | collective-permute-start | bytes 3145736 | tf_op jit(solution)/shard_map/ppermute | solution.py:38
  297.5 70.5 %collective-permute-start.21 = (bf16[512,4096]{1,0:T(8,128)(2,1)}, bf16[512,4096]{1,0:T(8,128)(2,1)}, u32[]{:S(2)}, u32[]{:S(2)}) collective-permute-start(bf16[512,4096]{1,0:T(8,128)(2,1)} %get-tuple-element.207.refs_33_), channel_id=1, source_target_pairs={{0,2},{2,0},{4,6},{6,4},{1,3},{3,1},{5,7},{7,5},{8,10},{10,8},{12,... | collective-permute-start | bytes 12582920 | tf_op jit(solution)/shard_map/ppermute | solution.py:38
  297.5 70.5 %collective-permute-start.20 = (bf16[512,4096]{1,0:T(8,128)(2,1)}, bf16[512,4096]{1,0:T(8,128)(2,1)}, u32[]{:S(2)}, u32[]{:S(2)}) collective-permute-start(bf16[512,4096]{1,0:T(8,128)(2,1)} %get-tuple-element.206.refs_32_), channel_id=1, source_target_pairs={{0,2},{2,0},{4,6},{6,4},{1,3},{3,1},{5,7},{7,5},{8,10},{10,8},{12,... | collective-permute-start | bytes 12582920 | tf_op jit(solution)/shard_map/ppermute | solution.py:38
  361.0 80.2 %collective-permute-start.22 = (bf16[512,2048]{1,0:T(8,128)(2,1)}, bf16[512,2048]{1,0:T(8,128)(2,1)}, u32[]{:S(2)}, u32[]{:S(2)}) collective-permute-start(bf16[512,2048]{1,0:T(8,128)(2,1)} %copy-done.32), channel_id=1, source_target_pairs={{0,1},{1,0},{2,3},{3,2},{4,5},{5,4},{6,7},{7,6},{8,9},{9,8},{10,11... | collective-permute-start | bytes 6291464 | tf_op jit(solution)/shard_map/ppermute | solution.py:38
  364.9 110.4 %collective-permute-start.26 = (bf16[2,512,4096]{2,1,0:T(8,128)(2,1)}, bf16[2,512,4096]{2,1,0:T(8,128)(2,1)}, u32[]{:S(2)}, u32[]{:S(2)}) collective-permute-start(bf16[2,512,4096]{2,1,0:T(8,128)(2,1)} %get-tuple-element.218.refs_32_), channel_id=1, source_target_pairs={{0,2},{2,0},{4,6},{6,4},{1,3},{3,1},{5,7},{7,5},{8,10},{10,8},{12,... | collective-permute-start | bytes 25165832 | tf_op jit(solution)/shard_map/ppermute | solution.py:38
  465.6 73.5 %collective-permute-start.31 = (bf16[512,2048]{1,0:T(8,128)(2,1)S(1)}, bf16[512,2048]{1,0:T(8,128)(2,1)}, u32[]{:S(2)}, u32[]{:S(2)}) collective-permute-start(bf16[512,2048]{1,0:T(8,128)(2,1)S(1)} %copy-done.29), channel_id=1, source_target_pairs={{0,1},{1,0},{2,3},{3,2},{4,5},{5,4},{6,7},{7,6},{8,9},{9,8},{10,11... | collective-permute-start | bytes 6291464 | tf_op jit(solution)/shard_map/ppermute | solution.py:38
  474.6 64.4 %collective-permute-start.29 = (bf16[128,4096]{1,0:T(8,128)(2,1)}, bf16[128,4096]{1,0:T(8,128)(2,1)}, u32[]{:S(2)}, u32[]{:S(2)}) collective-permute-start(bf16[128,4096]{1,0:T(8,128)(2,1)} %get-tuple-element.224), channel_id=1, source_target_pairs={{0,4},{2,6},{4,0},{6,2},{1,5},{3,7},{5,1},{7,3},{8,12},{10,14},{12... | collective-permute-start | bytes 3145736 | tf_op jit(solution)/shard_map/ppermute | solution.py:38
  597.6 64.0 %collective-permute-start.55 = (bf16[128,4096]{1,0:T(8,128)(2,1)S(1)}, bf16[128,4096]{1,0:T(8,128)(2,1)}, u32[]{:S(2)}, u32[]{:S(2)}) collective-permute-start(bf16[128,4096]{1,0:T(8,128)(2,1)S(1)} %copy-done.122), channel_id=1, source_target_pairs={{0,8},{8,0},{16,24},{24,16},{1,9},{9,1},{17,25},{25,17},{2,10},{10... | collective-permute-start | bytes 3145736 | tf_op jit(solution)/shard_map/ppermute | solution.py:38
  605.3 106.7 %collective-permute-start.54 = (bf16[128,4096]{1,0:T(8,128)(2,1)}, bf16[128,4096]{1,0:T(8,128)(2,1)}, u32[]{:S(2)}, u32[]{:S(2)}) collective-permute-start(bf16[128,4096]{1,0:T(8,128)(2,1)} %add_convert_fusion.15), channel_id=1, source_target_pairs={{0,8},{8,0},{16,24},{24,16},{1,9},{9,1},{17,25},{25,17},{2,10},{10... | collective-permute-start | bytes 3145736 | tf_op jit(solution)/shard_map/ppermute | solution.py:38
  620.7 92.0 %collective-permute-start.52 = (bf16[128,4096]{1,0:T(8,128)(2,1)}, bf16[128,4096]{1,0:T(8,128)(2,1)}, u32[]{:S(2)}, u32[]{:S(2)}) collective-permute-start(bf16[128,4096]{1,0:T(8,128)(2,1)} %add_convert_fusion.16), channel_id=1, source_target_pairs={{0,8},{8,0},{16,24},{24,16},{1,9},{9,1},{17,25},{25,17},{2,10},{10... | collective-permute-start | bytes 3145736 | tf_op jit(solution)/shard_map/ppermute | solution.py:38
  713.5 118.2 %collective-permute-start.59 = (bf16[1024,2048]{1,0:T(8,128)(2,1)}, bf16[1024,2048]{1,0:T(8,128)(2,1)}, u32[]{:S(2)}, u32[]{:S(2)}) collective-permute-start(bf16[1024,2048]{1,0:T(8,128)(2,1)} %bitcast.9.x_ref.refs_4_.refs_0_.refs_1_.refs_5_.refs_8_.refs_9_.refs_12_.refs_13_.refs_16_.refs_17_.refs_20_.refs_21, ...), channel_id=1, source_target_pairs={{0,2},{2,0},{4,6},{6,4},{1,3},{3,1},{5,7},{7,5},{8,10},{10,8},{12,... | collective-permute-start | bytes 12582920 | tf_op jit(solution)/shard_map/ppermute | solution.py:38
  807.8 62.9 %collective-permute-start.63 = (bf16[512,2048]{1,0:T(8,128)(2,1)S(1)}, bf16[512,2048]{1,0:T(8,128)(2,1)S(1)}, u32[]{:S(2)}, u32[]{:S(2)}) collective-permute-start(bf16[512,2048]{1,0:T(8,128)(2,1)S(1)} %copy-done.57), channel_id=1, source_target_pairs={{0,1},{1,0},{2,3},{3,2},{4,5},{5,4},{6,7},{7,6},{8,9},{9,8},{10,11... | collective-permute-start | bytes 6291464 | tf_op jit(solution)/shard_map/ppermute | solution.py:38
  831.7 68.5 %collective-permute-start.62 = (bf16[512,2048]{1,0:T(8,128)(2,1)S(1)}, bf16[512,2048]{1,0:T(8,128)(2,1)S(1)}, u32[]{:S(2)}, u32[]{:S(2)}) collective-permute-start(bf16[512,2048]{1,0:T(8,128)(2,1)S(1)} %copy-done.49), channel_id=1, source_target_pairs={{0,1},{1,0},{2,3},{3,2},{4,5},{5,4},{6,7},{7,6},{8,9},{9,8},{10,11... | collective-permute-start | bytes 6291464 | tf_op jit(solution)/shard_map/ppermute | solution.py:38
  855.0 76.8 %collective-permute-start.70 = (bf16[512,1024]{1,0:T(8,128)(2,1)}, bf16[512,1024]{1,0:T(8,128)(2,1)}, u32[]{:S(2)}, u32[]{:S(2)}) collective-permute-start(bf16[512,1024]{1,0:T(8,128)(2,1)} %get-tuple-element.288), channel_id=1, source_target_pairs={{0,4},{2,6},{4,0},{6,2},{1,5},{3,7},{5,1},{7,3},{8,12},{10,14},{12... | collective-permute-start | bytes 3145736 | tf_op jit(solution)/shard_map/ppermute | solution.py:38
  866.0 68.4 %collective-permute-start.67 = (bf16[512,1024]{1,0:T(8,128)(2,1)S(1)}, bf16[512,1024]{1,0:T(8,128)(2,1)S(1)}, u32[]{:S(2)}, u32[]{:S(2)}) collective-permute-start(bf16[512,1024]{1,0:T(8,128)(2,1)S(1)} %get-tuple-element.286), channel_id=1, source_target_pairs={{0,4},{2,6},{4,0},{6,2},{1,5},{3,7},{5,1},{7,3},{8,12},{10,14},{12... | collective-permute-start | bytes 3145736 | tf_op jit(solution)/shard_map/ppermute | solution.py:38
  866.8 68.0 %collective-permute-start.64 = (bf16[512,1024]{1,0:T(8,128)(2,1)S(1)}, bf16[512,1024]{1,0:T(8,128)(2,1)S(1)}, u32[]{:S(2)}, u32[]{:S(2)}) collective-permute-start(bf16[512,1024]{1,0:T(8,128)(2,1)S(1)} %get-tuple-element.284), channel_id=1, source_target_pairs={{0,4},{2,6},{4,0},{6,2},{1,5},{3,7},{5,1},{7,3},{8,12},{10,14},{12... | collective-permute-start | bytes 3145736 | tf_op jit(solution)/shard_map/ppermute | solution.py:38
  900.2 116.7 %collective-permute-start.82 = (bf16[128,4096]{1,0:T(8,128)(2,1)S(1)}, bf16[128,4096]{1,0:T(8,128)(2,1)S(1)}, u32[]{:S(2)}, u32[]{:S(2)}) collective-permute-start(bf16[128,4096]{1,0:T(8,128)(2,1)S(1)} %copy-done.146), channel_id=1, source_target_pairs={{0,16},{8,24},{16,0},{24,8},{1,17},{9,25},{17,1},{25,9},{2,18},{10... | collective-permute-start | bytes 3145736 | tf_op jit(solution)/shard_map/ppermute | solution.py:38
  929.6 85.6 %collective-permute-start.77 = (bf16[128,4096]{1,0:T(8,128)(2,1)S(1)}, bf16[128,4096]{1,0:T(8,128)(2,1)S(1)}, u32[]{:S(2)}, u32[]{:S(2)}) collective-permute-start(bf16[128,4096]{1,0:T(8,128)(2,1)S(1)} %copy-done.142), channel_id=1, source_target_pairs={{0,16},{8,24},{16,0},{24,8},{1,17},{9,25},{17,1},{25,9},{2,18},{10... | collective-permute-start | bytes 3145736 | tf_op jit(solution)/shard_map/ppermute | solution.py:38
  931.8 115.8 %collective-permute-start.76 = (bf16[128,4096]{1,0:T(8,128)(2,1)S(1)}, bf16[128,4096]{1,0:T(8,128)(2,1)S(1)}, u32[]{:S(2)}, u32[]{:S(2)}) collective-permute-start(bf16[128,4096]{1,0:T(8,128)(2,1)S(1)} %copy-done.141), channel_id=1, source_target_pairs={{0,16},{8,24},{16,0},{24,8},{1,17},{9,25},{17,1},{25,9},{2,18},{10... | collective-permute-start | bytes 3145736 | tf_op jit(solution)/shard_map/ppermute | solution.py:38
  934.4 117.0 %collective-permute-start.79 = (bf16[128,4096]{1,0:T(8,128)(2,1)S(1)}, bf16[128,4096]{1,0:T(8,128)(2,1)S(1)}, u32[]{:S(2)}, u32[]{:S(2)}) collective-permute-start(bf16[128,4096]{1,0:T(8,128)(2,1)S(1)} %add_convert_fusion.7), channel_id=1, source_target_pairs={{0,8},{8,0},{16,24},{24,16},{1,9},{9,1},{17,25},{25,17},{2,10},{10... | collective-permute-start | bytes 3145736 | tf_op jit(solution)/shard_map/ppermute | solution.py:38
  934.8 112.8 %collective-permute-start.80 = (bf16[128,4096]{1,0:T(8,128)(2,1)S(1)}, bf16[128,4096]{1,0:T(8,128)(2,1)S(1)}, u32[]{:S(2)}, u32[]{:S(2)}) collective-permute-start(bf16[128,4096]{1,0:T(8,128)(2,1)S(1)} %add_convert_fusion.4), channel_id=1, source_target_pairs={{0,8},{8,0},{16,24},{24,16},{1,9},{9,1},{17,25},{25,17},{2,10},{10... | collective-permute-start | bytes 3145736 | tf_op jit(solution)/shard_map/ppermute | solution.py:38
  1016.9 72.0 %collective-permute-start.78 = (bf16[128,4096]{1,0:T(8,128)(2,1)S(1)}, bf16[128,4096]{1,0:T(8,128)(2,1)S(1)}, u32[]{:S(2)}, u32[]{:S(2)}) collective-permute-start(bf16[128,4096]{1,0:T(8,128)(2,1)S(1)} %add_convert_fusion.9), channel_id=1, source_target_pairs={{0,4},{2,6},{4,0},{6,2},{1,5},{3,7},{5,1},{7,3},{8,12},{10,14},{12... | collective-permute-start | bytes 3145736 | tf_op jit(solution)/shard_map/ppermute | solution.py:38
  1051.3 71.1 %collective-permute-start.81 = (bf16[128,4096]{1,0:T(8,128)(2,1)S(1)}, bf16[128,4096]{1,0:T(8,128)(2,1)S(1)}, u32[]{:S(2)}, u32[]{:S(2)}) collective-permute-start(bf16[128,4096]{1,0:T(8,128)(2,1)S(1)} %add_convert_fusion.3), channel_id=1, source_target_pairs={{0,16},{8,24},{16,0},{24,8},{1,17},{9,25},{17,1},{25,9},{2,18},{10... | collective-permute-start | bytes 3145736 | tf_op jit(solution)/shard_map/ppermute | solution.py:38
  (213 other events, 4794.0 us)
